TPU v7x, 32 devices: a whole 2x2x4 slice. The times are simulated.
32 devices in a mesh: tile: 16 (over z, y, x), slide: 2 (over core).
Axes of the slice: x: 2, y: 2, z: 4, core: 2. Of those that a mesh axis runs over, the one named last changes fastest.
Arguments:
- features: bfloat16 [64, 32, 32, 256], P(('slide', 'tile')), parts along dimension 0, may hold values from -8 to 8
- neighbours: int32 [64, 8], P(('slide', 'tile')), parts along dimension 0, may hold values from 0 to 32, as said below
- conv_weight: bfloat16 [3, 3, 256, 256], replicated, may hold values from -0.125 to 0.125
- patch_weight: bfloat16 [4096, 768], replicated, may hold values from -1 to 1
- query_weight: bfloat16 [768, 768], replicated, may hold values from -2 to 2
- key_weight: bfloat16 [768, 768], replicated, may hold values from -2 to 2
- value_weight: bfloat16 [768, 768], replicated, may hold values from -0.21875 to 0.21875
- output_weight: bfloat16 [768, 768], replicated, may hold values from -0.21875 to 0.21875
- cotangent: bfloat16 [4096, 768], P(('slide', 'tile')), parts along dimension 0, may hold values from -6 to 6
Outputs:
- mixed: bfloat16 [4096, 768], P(('slide', 'tile')), parts along dimension 0
- output_grad: float32 [1536, 768], P('slide'), parts along dimension 0
There are 2 independent parts, one for each index of `slide`. A program takes and returns all parts, laid end to end along the dimension named above; an argument that names none is the same for every part. Nothing has to cross between parts.
Inputs may be any that keep to these rules, and one draw needn't show every extreme that they name: Tiles are tissue cells of a grid 16 cells wide; the tile numbers are given to the tissue cells in a drawn order, so neighbours may have any numbers; each entry is the index of the tissue tile at that grid offset, or 32.
All inputs are finite; a program needn't handle non-finite values.
Results may differ from a plain program's by a relative error of at most 0.02.
Values may be sent and summed in bfloat16 or wider, within the bound.
A program may use at most 192 MiB of HBM per device.

v0:
```python
import jax
import jax.numpy as jnp
from jax import lax
from jax.sharding import PartitionSpec as P

PATCH = 4
HEADS = 12
HD = 64


def tile_faces(maps):
    return jnp.stack([maps[:, 0], maps[:, -1], maps[:, :, 0], maps[:, :, -1]], axis=1)


def pad_tiles(maps, all_faces, links):
    upper = all_faces[links[:, 1], 1]
    lower = all_faces[links[:, 6], 0]
    left_col = all_faces[links[:, 3], 3]
    right_col = all_faces[links[:, 4], 2]
    corner_ul = all_faces[links[:, 0], 1, -1]
    corner_ur = all_faces[links[:, 2], 1, 0]
    corner_dl = all_faces[links[:, 5], 0, -1]
    corner_dr = all_faces[links[:, 7], 0, 0]
    top_row = jnp.concatenate([corner_ul[:, None], upper, corner_ur[:, None]], axis=1)
    bottom_row = jnp.concatenate([corner_dl[:, None], lower, corner_dr[:, None]], axis=1)
    middle = jnp.concatenate([left_col[:, :, None], maps, right_col[:, :, None]], axis=2)
    return jnp.concatenate([top_row[:, None], middle, bottom_row[:, None]], axis=1)


def conv_tiles(padded, kernel):
    count = padded.shape[0]
    side = padded.shape[1] - 2
    chans = padded.shape[3]
    total = jnp.zeros((count * side * side, kernel.shape[3]), jnp.float32)
    for row_off in range(3):
        for col_off in range(3):
            window = padded[:, row_off : row_off + side, col_off : col_off + side, :].reshape(
                -1, chans
            )
            total = total + jnp.dot(
                window, kernel[row_off, col_off], preferred_element_type=jnp.float32
            )
    return jax.nn.gelu(total).astype(jnp.bfloat16).reshape(count, side, side, -1)


def patchify(hidden, patch):
    count, side, _, chans = hidden.shape
    blocks = side // patch
    grid = hidden.reshape(count, blocks, patch, blocks, patch, chans).transpose(0, 1, 3, 2, 4, 5)
    return grid.reshape(count * blocks * blocks, patch * patch * chans)


def local(
    features,
    neighbours,
    conv_weight,
    patch_weight,
    query_weight,
    key_weight,
    value_weight,
    output_weight,
    cotangent,
):
    local_faces = tile_faces(features)
    gathered = lax.all_gather(local_faces, "tile", axis=0, tiled=True)
    all_faces = jnp.concatenate(
        [gathered, jnp.zeros((1,) + gathered.shape[1:], jnp.bfloat16)], axis=0
    )
    padded = pad_tiles(features, all_faces, neighbours)
    hidden = conv_tiles(padded, conv_weight)
    tokens = jnp.dot(
        patchify(hidden, PATCH), patch_weight, preferred_element_type=jnp.float32
    ).astype(jnp.bfloat16)
    rows = tokens.shape[0]
    query = (
        jnp.dot(tokens, query_weight, preferred_element_type=jnp.float32)
        .astype(jnp.bfloat16)
        .reshape(rows, HEADS, HD)
    )
    scale = HD ** (-0.5)
    keys = jnp.dot(tokens, key_weight, preferred_element_type=jnp.float32).astype(jnp.bfloat16)
    values = jnp.dot(tokens, value_weight, preferred_element_type=jnp.float32).astype(jnp.bfloat16)
    top = jnp.full((HEADS, rows), -1e30, jnp.float32)
    key_heads = lax.all_gather(keys, "tile", axis=0, tiled=True).reshape(-1, HEADS, HD)
    value_heads = lax.all_gather(values, "tile", axis=0, tiled=True).reshape(-1, HEADS, HD)
    scores = (
        jnp.einsum("qhd,khd->hqk", query, key_heads, preferred_element_type=jnp.float32) * scale
    )
    new_top = jnp.maximum(top, jnp.max(scores, axis=-1))
    weights = jnp.exp(scores - new_top[..., None])
    total = jnp.sum(weights, axis=-1)
    accum = jnp.einsum(
        "hqk,khd->hqd",
        weights.astype(jnp.bfloat16),
        value_heads,
        preferred_element_type=jnp.float32,
    )
    top, total, accum = (new_top, total, accum)
    attended = (
        (accum / total[..., None]).transpose(1, 0, 2).reshape(rows, HEADS * HD).astype(jnp.bfloat16)
    )
    mixed = (
        tokens.astype(jnp.float32)
        + jnp.dot(attended, output_weight, preferred_element_type=jnp.float32)
    ).astype(jnp.bfloat16)
    grad_term = jnp.dot(attended.T, cotangent, preferred_element_type=jnp.float32)
    output_grad = lax.psum(grad_term, "tile")
    return (mixed, output_grad)


def solution(mesh):
    in_specs = (
        P(("slide", "tile"), None, None, None),
        P(("slide", "tile"), None),
        P(),
        P(),
        P(),
        P(),
        P(),
        P(),
        P(("slide", "tile"), None),
    )
    out_specs = (P(("slide", "tile"), None), P("slide", None))
    return jax.shard_map(local, mesh=mesh, in_specs=in_specs, out_specs=out_specs, check_vma=False)
```

profile of v0, /device:TPU:0, one launch (start us, length us, event | category | flops | bytes accessed | tf_op | source)
XLA Modules:
  0.0 401.6 jit_solution(3821570534469536832)
XLA Ops:
  11.3 63.5 %all-gather.4.cloned.1.call-done = bf16[32,4,32,256]{3,2,1,0:T(8,128)(2,1)} async-done(((bf16[2,4,32,256]{3,2,1,0:T(8,128)(2,1)}), bf16[32,4,32,256]{3,2,1,0:T(8,128)(2,1)}) %all-gather.4.cloned.1.call-update) | async-done | bytes 2097168 | tf_op jit(solution)/shard_map/all_gather | solution.py:65
  74.8 3.2 concatenate.53
  78.0 2.2 gather_fusion.1
  80.2 1.5 gather_fusion
  81.7 1.5 gather_fusion.2
  83.2 2.2 gather_fusion.6
  85.3 1.5 gather_fusion.5
  88.3 2.2 gather_fusion.3
  90.5 2.2 gather_fusion.4
  94.0 1.7 pad_maximum_fusion
  103.9 1.8 reshape.58
  105.8 3.8 convolution_convert_fusion.3
  110.6 2.3 convolution_convert_fusion
  113.7 63.9 %all-gather.6.cloned.1.call-done = bf16[2048,768]{1,0:T(8,128)(2,1)} async-done(((bf16[128,768]{1,0:T(8,128)(2,1)}), bf16[2048,768]{1,0:T(8,128)(2,1)}) %all-gather.6.cloned.1.call-update) | async-done | bytes 3145744 | tf_op jit(solution)/shard_map/all_gather | solution.py:84
  177.6 4.7 %copy.53 = bf16[2048,768]{0,1:T(8,128)(2,1)} copy(bf16[2048,768]{1,0:T(8,128)(2,1)} %all-gather.6.cloned.1.call-done) | data formatting | bytes 6291456 | tf_op jit(solution)/shard_map/all_gather | solution.py:84
  182.3 3.8 multiply_reduce_fusion
  186.2 4.6 %copy-done.2 = f32[12,128,2048]{2,1,0:T(8,128)} copy-done((f32[12,128,2048]{2,1,0:T(8,128)}, f32[12,128,2048]{2,1,0:T(8,128)S(1)}, u32[]{:S(2)}) %copy-start.2) | copy-done | bytes 12582936
  190.7 2.4 fusion
  193.2 54.5 %all-gather.8.cloned.1.call-done = bf16[2048,768]{1,0:T(8,128)(2,1)} async-done(((bf16[128,768]{1,0:T(8,128)(2,1)}), bf16[2048,768]{1,0:T(8,128)(2,1)}) %all-gather.8.cloned.1.call-update) | async-done | bytes 3145744 | tf_op jit(solution)/shard_map/all_gather | solution.py:85
  247.6 4.7 %copy.54 = bf16[2048,768]{0,1:T(8,128)(2,1)} copy(bf16[2048,768]{1,0:T(8,128)(2,1)} %all-gather.8.cloned.1.call-done) | data formatting | bytes 6291456 | tf_op jit(solution)/shard_map/all_gather | solution.py:85
  252.3 7.9 %fusion.21 = bf16[128,12,64]{0,2,1:T(8,128)(2,1)S(1)} fusion(bf16[2048,12,64]{0,2,1:T(8,128)(2,1)} %bitcast.102, f32[12,128,2048]{2,1,0:T(8,128)} %copy-done.2, f32[12,128]{1,0:T(8,128)S(1)} %broadcast_maximum_fusion, f32[128,12]{0,1:T(8,128)S(1)} %bitcast.109), kind=kOutput, calls=%fused_computation.45 | convolution fusion | flops 412286976 | bytes 15937536 | tf_op jit(solution)/shard_map/hqk,khd->hqd/dot_general | solution.py:92
  260.3 1.9 fusion.79
  263.2 128.5 %all-reduce.8.cloned.1.call-done = f32[768,768]{1,0:T(8,128)} async-done(((f32[768,768]{1,0:T(8,128)}), f32[768,768]{1,0:T(8,128)}) %all-reduce.8.cloned.1.call-update) | async-done | bytes 2359312 | tf_op jit(solution)/shard_map/psum | solution.py:107
  391.8 3.2 copy.62
  (56 shorter events, 17.9 us)
Async XLA Ops:
  7.2 102.4 %copy-start = (bf16[768,768]{1,0:T(8,128)(2,1)S(1)}, bf16[768,768]{1,0:T(8,128)(2,1)}, u32[]{:S(2)}) copy-start(bf16[768,768]{1,0:T(8,128)(2,1)} %param.14) | copy-start | bytes 3538948
  7.2 67.6 %all-gather.4.cloned.1.call-start = ((), (), s32[]{:S(2)}) async-start(), calls=%async_computation | async-start | bytes 2228224 | tf_op jit(solution)/shard_map/all_gather | solution.py:65
  10.0 167.7 %all-gather.6.cloned.1.call-start = ((), (), s32[]{:S(2)}) async-start(), calls=%async_computation.1 | async-start | bytes 3342336 | tf_op jit(solution)/shard_map/all_gather | solution.py:84
  11.3 81.5 %copy-start.3 = (bf16[2,32,32,256]{3,2,1,0:T(8,128)(2,1)S(1)}, bf16[2,32,32,256]{3,2,1,0:T(8,128)(2,1)}, u32[]{:S(2)}) copy-start(bf16[2,32,32,256]{3,2,1,0:T(8,128)(2,1)} %param.9) | copy-start | bytes 3145732
  96.5 1.3 copy-start.6
  109.5 3.6 copy-start.4
  110.6 137.0 %all-gather.8.cloned.1.call-start = ((), (), s32[]{:S(2)}) async-start(), calls=%async_computation.2 | async-start | bytes 3342336 | tf_op jit(solution)/shard_map/all_gather | solution.py:85
  112.9 278.8 %all-reduce.8.cloned.1.call-start = ((), (), s32[]{:S(2)}) async-start(), calls=%async_computation.3 | async-start | bytes 4718592 | tf_op jit(solution)/shard_map/psum | solution.py:107
  186.1 4.6 %copy-start.2 = (f32[12,128,2048]{2,1,0:T(8,128)}, f32[12,128,2048]{2,1,0:T(8,128)S(1)}, u32[]{:S(2)}) copy-start(f32[12,128,2048]{2,1,0:T(8,128)S(1)} %get-tuple-element.25) | copy-start | bytes 37748740
  252.3 8.0 %copy-start.7 = (bf16[128,768]{1,0:T(8,128)(2,1)S(1)}, bf16[128,768]{1,0:T(8,128)(2,1)}, u32[]{:S(2)}) copy-start(bf16[128,768]{1,0:T(8,128)(2,1)} %param.17) | copy-start | bytes 589828
  260.3 1.9 copy-start.5
  262.2 132.8 %copy-start.1 = (bf16[768,768]{1,0:T(8,128)(2,1)S(1)}, bf16[768,768]{1,0:T(8,128)(2,1)}, u32[]{:S(2)}) copy-start(bf16[768,768]{1,0:T(8,128)(2,1)} %param.14) | copy-start | bytes 3538948
Sparse Core Ops, SparseCore 0:
  11.4 63.3 all-gather.3
  110.7 66.8 all-gather.5
  181.0 66.5 all-gather.7
  262.3 129.4 all-reduce.7
where the time goes:
time: 402 us
  waiting for transfers between devices  311 us (77%)
  local copies, waits for them, and re-layouts  42.8 us (11%)
  matrix products  26.5 us (7%)
  between operations  14.1 us (4%)
  other arithmetic  7.32 us (2%)
    psum x1, waiting for transfers between devices, local(): output_grad = lax.psum(grad_term, 'tile')  129 us
    all_gather x1, waiting for transfers between devices, local(): lax.all_gather(keys, 'tile', axis=0, tiled=True).reshape(-1, HEADS, HD)  63.9 us
    all_gather x1, waiting for transfers between devices, local(): gathered = lax.all_gather(local_faces, 'tile', axis=0, tiled=True)  63.5 us
    all_gather x1, waiting for transfers between devices, local(): lax.all_gather(values, 'tile', axis=0, tiled=True).reshape(-1, HEADS, HD)  54.5 us
    unnamed x17, local copies, waits for them, and re-layouts  8.31 us
  transfers between devices with their start and end apart: 4, of which 4 were waited for; matrix products, arithmetic and copies ran while one was open for 4% of the time, Pallas kernels for 0%

commit v1 on v0

v1 whole, which is shorter than its diff:
```python
import functools
import math

import jax
import jax.numpy as jnp
from jax import lax
from jax.experimental import pallas as pl
from jax.experimental.pallas import tpu as pltpu
from jax.sharding import PartitionSpec as P

PATCH = 4
HEADS = 12
HD = 64
GROUP = 4
GH = HEADS // GROUP
GW = GH * HD
MESH = pl.DeviceIdType.MESH
F32 = jnp.float32
BF16 = jnp.bfloat16


def remote(src, dst, send, recv, device):
    return pltpu.make_async_remote_copy(
        src_ref=src,
        dst_ref=dst,
        send_sem=send,
        recv_sem=recv,
        device_id={"tile": device},
        device_id_type=MESH,
    )


def place():
    me = lax.axis_index("tile")
    return me, me // GROUP, me % GROUP


def plane_partners(p):
    px = p + 1 - 2 * (p % 2)
    py = p + 2 - 4 * (p // 2)
    return px, py, GROUP - 1 - p


def when(cond, body):
    if isinstance(cond, bool):
        if cond:
            body()
    else:
        pl.when(cond)(body)


def stage_blocks(c, cols, s):
    if s == 0:
        return [(c, True, True, True)]
    return [(c - s, c - s >= 0, True, False), (c + s, c + s < cols, False, True)]


def gather_all(buf, cols, ss, rs):
    me, c, p = place()
    px, py, pd = plane_partners(p)

    def full(k, q):
        return buf.at[pl.ds(2 * (k * GROUP + q), 2)]

    def half(k, q, h):
        return buf.at[2 * (k * GROUP + q) + h]

    def z_copy(k, d):
        to = c + 1 - 2 * d
        return remote(full(k, p), full(k, p), ss.at[d, k], rs.at[0, k], to * GROUP + p)

    def x_copy(k, q):
        return remote(full(k, q), full(k, q), ss.at[2, k], rs.at[1, k], c * GROUP + px)

    def y_copy(k, q):
        return remote(full(k, q), full(k, q), ss.at[3, k], rs.at[2, k], c * GROUP + py)

    def y_pass(k, q):
        return remote(half(k, q, 0), half(k, q, 0), ss.at[4, k], rs.at[3, k], c * GROUP + py)

    def x_pass(k, q):
        return remote(half(k, q, 1), half(k, q, 1), ss.at[5, k], rs.at[4, k], c * GROUP + px)

    def pass_on(s):
        for k, ok, _, _ in stage_blocks(c, cols, s):
            def body(k=k):
                x_copy(k, px).wait_recv()
                y_pass(k, px).start()
                y_copy(k, py).wait_recv()
                x_pass(k, py).start()
            when(ok, body)

    for s in range(cols):
        for k, ok, up, down in stage_blocks(c, cols, s):
            def body(k=k, up=up, down=down):
                if s > 0:
                    z_copy(k, 0).wait_recv()
                if s < cols - 1:
                    if up:
                        when(c + 1 < cols, lambda: z_copy(k, 0).start())
                    if down:
                        when(c >= 1, lambda: z_copy(k, 1).start())
                x_copy(k, p).start()
                y_copy(k, p).start()
            when(ok, body)
        if s > 0:
            pass_on(s - 1)
    pass_on(cols - 1)
    for k in range(cols):
        y_pass(k, pd).wait_recv()
        x_pass(k, pd).wait_recv()
    for s in range(cols):
        for k, ok, up, down in stage_blocks(c, cols, s):
            def body(k=k, up=up, down=down):
                if s < cols - 1:
                    if up:
                        when(c + 1 < cols, lambda: z_copy(k, 0).wait_send())
                    if down:
                        when(c >= 1, lambda: z_copy(k, 1).wait_send())
                x_copy(k, p).wait_send()
                y_copy(k, p).wait_send()
                y_pass(k, px).wait_send()
                x_pass(k, py).wait_send()
            when(ok, body)


def embed_kernel(
    cols, x_ref, own_ref, nb_ref, cw_ref, pw_hbm, wq_hbm, wk_hbm, wv_hbm,
    tok_ref, kv_ref, q_ref,
    faces, ep, pw, ww, ss, rs, local_sem,
):
    n = cols * GROUP
    me, c, p = place()
    px, py, pd = plane_partners(p)
    loads = [
        pltpu.make_async_copy(x_ref, ep.at[pl.ds(1, 4), pl.ds(1, 4)], local_sem.at[0]),
        pltpu.make_async_copy(pw_hbm, pw, local_sem.at[1]),
        pltpu.make_async_copy(wq_hbm, ww.at[0], local_sem.at[2]),
        pltpu.make_async_copy(wk_hbm, ww.at[1], local_sem.at[3]),
        pltpu.make_async_copy(wv_hbm, ww.at[2], local_sem.at[4]),
    ]
    for load in loads:
        load.start()
    barrier = pltpu.get_barrier_semaphore()
    pl.semaphore_signal(barrier, inc=1, device_id={"tile": c * GROUP + px}, device_id_type=MESH)
    pl.semaphore_signal(barrier, inc=1, device_id={"tile": c * GROUP + py}, device_id_type=MESH)

    @pl.when(c + 1 < cols)
    def _():
        pl.semaphore_signal(barrier, inc=1, device_id={"tile": me + GROUP}, device_id_type=MESH)

    @pl.when(c >= 1)
    def _():
        pl.semaphore_signal(barrier, inc=1, device_id={"tile": me - GROUP}, device_id_type=MESH)

    faces[pl.ds(2 * me, 2)] = own_ref[...]
    faces[2 * n] = jnp.zeros_like(faces[2 * n])
    inner = (c >= 1) & (c + 1 < cols)

    @pl.when(inner)
    def _():
        pl.semaphore_wait(barrier, 4)

    @pl.when(jnp.logical_not(inner))
    def _():
        pl.semaphore_wait(barrier, 3)

    gather_all(faces, cols, ss, rs)

    loads[0].wait()
    ch = ep.shape[3]
    first = lax.broadcasted_iota(jnp.int32, (64, ch), 0) % 8

    def spread(col):
        return jnp.broadcast_to(col[:, None, :], (8, 8, ch)).reshape(64, ch)

    for t in range(2):
        rows = pl.ds(t * 64, 64)

        def face(link, which):
            return faces[nb_ref[t, link], which].astype(F32)

        upper = face(1, 1)
        lower = face(6, 0)
        left = face(3, 3)
        right = face(4, 2)
        corner_ul = face(0, 1)[31:32]
        corner_ur = face(2, 1)[0:1]
        corner_dl = face(5, 0)[31:32]
        corner_dr = face(7, 0)[0:1]
        for b in range(4):
            part = slice(b * 8, b * 8 + 8)
            above = jnp.concatenate([upper[part], ep[4, b + 1, rows].astype(F32)[0:56]], axis=0)
            below = jnp.concatenate([ep[1, b + 1, rows].astype(F32)[8:64], lower[part]], axis=0)
            ep[0, b + 1, rows] = above.astype(BF16)
            ep[5, b + 1, rows] = below.astype(BF16)
        lefts = [jnp.concatenate([corner_ul, left[24:31]], axis=0)]
        rights = [jnp.concatenate([corner_ur, right[24:31]], axis=0)]
        for a in range(4):
            lefts.append(left[a * 8:a * 8 + 8])
            rights.append(right[a * 8:a * 8 + 8])
        lefts.append(jnp.concatenate([left[1:8], corner_dl], axis=0))
        rights.append(jnp.concatenate([right[1:8], corner_dr], axis=0))
        for a in range(6):
            west = pltpu.roll(ep[a, 4, rows].astype(F32), 1, 0)
            east = pltpu.roll(ep[a, 1, rows].astype(F32), 63, 0)
            ep[a, 0, rows] = jnp.where(first == 0, spread(lefts[a]), west).astype(BF16)
            ep[a, 5, rows] = jnp.where(first == 7, spread(rights[a]), east).astype(BF16)

    loads[1].wait()
    tok = jnp.zeros(tok_ref.shape, F32)
    for i in range(4):
        acc = jnp.zeros((512, ch), F32)
        for dy in range(3):
            for dx in range(3):
                acc = acc + jnp.dot(
                    ep[i + dy, dx:dx + 4].reshape(512, ch), cw_ref[dy * 3 + dx],
                    preferred_element_type=F32,
                )
        hidden = jax.nn.gelu(acc).astype(BF16)
        wide = jnp.concatenate([hidden[j * 128:(j + 1) * 128] for j in range(4)], axis=1)
        tok = tok + jnp.dot(
            wide, pw[i * 4 * ch:(i + 1) * 4 * ch], preferred_element_type=F32
        )
    tokens = tok.astype(BF16)
    tok_ref[...] = tokens
    for load in loads[2:]:
        load.wait()
    query = jnp.dot(tokens, ww[0], preferred_element_type=F32)
    keys = jnp.dot(tokens, ww[1], preferred_element_type=F32)
    values = jnp.dot(tokens, ww[2], preferred_element_type=F32)
    for g in range(GROUP):
        part = slice(g * GW, (g + 1) * GW)
        q_ref[g] = query[:, part].astype(BF16)
        kv_ref[g] = jnp.concatenate([keys[:, part], values[:, part]], axis=1).astype(BF16)


def attend_kernel(
    cols, own_rows, tok_ref, kv_ref, q_ref, cot_ref, wo_ref,
    mixed_ref, grad_ref,
    kvg, qg, og, ogr, cotg, part_f, part_s, part_r, gr,
    kv_ss, kv_rs, q_ss, q_rs, c_ss, c_rs, o_ss, o_rs, z_ss, z_rs, p_ss, p_rs, ss, rs,
):
    n = cols * GROUP
    owners = GW // own_rows
    me, c, p = place()
    barrier = pltpu.get_barrier_semaphore()
    for d in range(1, GROUP):
        pl.semaphore_signal(
            barrier, inc=1, device_id={"tile": c * GROUP + (p + d) % GROUP}, device_id_type=MESH
        )
    for d in range(1, cols):
        pl.semaphore_signal(
            barrier, inc=1, device_id={"tile": (c + d) % cols * GROUP + p}, device_id_type=MESH
        )
    kvg[me] = kv_ref[p]
    qg[p] = q_ref[p]
    cotg[p] = cot_ref[...]
    pl.semaphore_wait(barrier, GROUP - 1 + cols - 1)

    def kv_plane(d):
        g = (p + d) % GROUP
        return remote(kv_ref.at[g], kvg.at[me], kv_ss.at[d], kv_rs.at[d], c * GROUP + g)

    def q_plane(d):
        g = (p + d) % GROUP
        return remote(q_ref.at[g], qg.at[p], q_ss.at[d], q_rs.at[d], c * GROUP + g)

    def c_plane(d):
        g = (p + d) % GROUP
        return remote(cotg.at[p], cotg.at[p], c_ss.at[d], c_rs.at[d], c * GROUP + g)

    def z_copy(k, d, way):
        b = k * GROUP + (p + GROUP - d) % GROUP
        to = c + 1 - 2 * way
        return remote(kvg.at[b], kvg.at[b], z_ss.at[way, k, d], z_rs.at[k, d], to * GROUP + p)

    for d in range(1, GROUP):
        kv_plane(d).start()
    for d in range(1, GROUP):
        q_plane(d).start()
    for s in range(cols):
        for d in range(GROUP):
            for k, ok, up, down in stage_blocks(c, cols, s):
                def body(k=k, up=up, down=down):
                    if s > 0:
                        z_copy(k, d, 0).wait_recv()
                    elif d > 0:
                        kv_plane(d).wait_recv()
                    if s < cols - 1:
                        if up:
                            when(c + 1 < cols, lambda: z_copy(k, d, 0).start())
                        if down:
                            when(c >= 1, lambda: z_copy(k, d, 1).start())
                when(ok, body)
        if s == 0:
            for d in range(1, GROUP):
                c_plane(d).start()
    for d in range(1, GROUP):
        q_plane(d).wait_recv()

    factor = HD ** (-0.5) * math.log2(math.e)

    def o_plane(d):
        g = (p + d) % GROUP
        return remote(og.at[g], ogr.at[p], o_ss.at[d], o_rs.at[d], c * GROUP + g)

    def attend(i, carry):
        g = (p + 1 + i) % GROUP
        for h in range(GH):
            lanes = slice(h * HD, (h + 1) * HD)
            key = kvg[:, :, lanes].reshape(n * 128, HD)
            value = kvg[:, :, GW + h * HD:GW + (h + 1) * HD].reshape(n * 128, HD)
            query = qg[g, :, lanes]
            scores = lax.dot_general(
                query, key, (((1,), (1,)), ((), ())), preferred_element_type=F32
            )
            top = jnp.max(scores, axis=1, keepdims=True)
            weights = jnp.exp2((scores - top) * factor)
            total = jnp.sum(weights, axis=1, keepdims=True)
            out = jnp.dot(weights.astype(BF16), value, preferred_element_type=F32)
            og[g, :, lanes] = (out / total).astype(BF16)

        return carry

    lax.fori_loop(0, GROUP, attend, 0)
    for d in range(1, GROUP):
        o_plane(d).start()
    for d in range(1, GROUP):
        c_plane(d).wait_recv()
    part = lax.dot_general(
        og[...].reshape(GROUP * 128, GW), cotg[...].reshape(GROUP * 128, -1),
        (((0,), (0,)), ((), ())), preferred_element_type=F32,
    )
    part_f[...] = part.reshape(part_f.shape)
    part_s[...] = part.reshape(part_f.shape).astype(BF16)

    def p_copy(d):
        j = (c + d) % cols
        return j, remote(
            part_s.at[j], part_r.at[d], p_ss.at[d], p_rs.at[d], j * GROUP + p
        )

    for d in range(1, cols):
        j, copy = p_copy(d)
        when(j < owners if owners < cols else True, copy.start)
    ogr[p] = og[p]
    for d in range(1, GROUP):
        o_plane(d).wait_recv()
    total = tok_ref[...].astype(F32)
    for g in range(GROUP):
        total = total + jnp.dot(
            ogr[g], wo_ref[g * GW:(g + 1) * GW], preferred_element_type=F32
        )
    mixed_ref[...] = total.astype(BF16)

    def reduce():
        acc = part_f[c]
        for d in range(1, cols):
            p_copy(d)[1].wait_recv()
            acc = acc + part_r[d].astype(F32)
        wide = acc.shape[1] // 2
        gr[2 * me] = acc[:, :wide].astype(BF16)
        gr[2 * me + 1] = acc[:, wide:].astype(BF16)

    def nothing():
        gr[2 * me] = jnp.zeros(gr.shape[1:], BF16)
        gr[2 * me + 1] = jnp.zeros(gr.shape[1:], BF16)

    if owners < cols:
        pl.when(c < owners)(reduce)
        pl.when(c >= owners)(nothing)
    else:
        reduce()
    gather_all(gr, cols, ss, rs)
    grad_ref[...] = gr[...]

    for d in range(1, GROUP):
        kv_plane(d).wait_send()
        q_plane(d).wait_send()
        c_plane(d).wait_send()
        o_plane(d).wait_send()
    for d in range(1, cols):
        j, copy = p_copy(d)
        when(j < owners if owners < cols else True, copy.wait_send)
    for s in range(cols - 1):
        for d in range(GROUP):
            for k, ok, up, down in stage_blocks(c, cols, s):
                def body(k=k, up=up, down=down):
                    if up:
                        when(c + 1 < cols, lambda: z_copy(k, d, 0).wait_send())
                    if down:
                        when(c >= 1, lambda: z_copy(k, d, 1).wait_send())
                when(ok, body)


def local(
    n, features, neighbours, conv_weight, patch_weight, query_weight, key_weight,
    value_weight, output_weight, cotangent,
):
    cols = n // GROUP
    tiles, side, _, ch = features.shape
    blocks = side // PATCH
    dm = query_weight.shape[0]
    rows = tiles * blocks * blocks
    vmem = pl.BlockSpec(memory_space=pltpu.VMEM)
    anyw = pl.BlockSpec(memory_space=pl.ANY)
    dma = pltpu.SemaphoreType.DMA

    x = features.reshape(tiles, blocks, PATCH, blocks, PATCH, ch).transpose(2, 4, 0, 1, 3, 5)
    own = jnp.stack(
        [
            x[0, :, :, 0].transpose(1, 0, 2, 3),
            x[-1, :, :, -1].transpose(1, 0, 2, 3),
            x[:, 0, :, :, 0].transpose(1, 0, 2, 3),
            x[:, -1, :, :, -1].transpose(1, 0, 2, 3),
        ],
        axis=1,
    ).reshape(tiles, 4, side, ch)
    x = x.reshape(PATCH, PATCH, rows, ch)

    tok, kv, q = pl.pallas_call(
        functools.partial(embed_kernel, cols),
        out_shape=(
            jax.ShapeDtypeStruct((rows, dm), BF16),
            jax.ShapeDtypeStruct((GROUP, rows, 2 * GW), BF16),
            jax.ShapeDtypeStruct((GROUP, rows, GW), BF16),
        ),
        in_specs=[anyw, vmem, pl.BlockSpec(memory_space=pltpu.SMEM), vmem, anyw, anyw, anyw, anyw],
        out_specs=(vmem, vmem, vmem),
        scratch_shapes=[
            pltpu.VMEM((2 * n + 1, 4, side, ch), BF16),
            pltpu.VMEM((6, 6, rows, ch), BF16),
            pltpu.VMEM(patch_weight.shape, BF16),
            pltpu.VMEM((3, dm, dm), BF16),
            dma((6, cols)),
            dma((5, cols)),
            dma((5,)),
        ],
        compiler_params=pltpu.CompilerParams(
            collective_id=0, has_side_effects=True, vmem_limit_bytes=52 * 2**20
        ),
        name="embed",
    )(
        x, own, neighbours, conv_weight.reshape(9, ch, ch), patch_weight,
        query_weight, key_weight, value_weight,
    )

    own_rows = max(16, GW // cols // 16 * 16)
    owners = GW // own_rows
    mixed, grad = pl.pallas_call(
        functools.partial(attend_kernel, cols, own_rows),
        out_shape=(
            jax.ShapeDtypeStruct((rows, dm), BF16),
            jax.ShapeDtypeStruct((2 * n, own_rows, dm // 2), BF16),
        ),
        in_specs=[vmem] * 5,
        out_specs=(vmem, vmem),
        scratch_shapes=[
            pltpu.VMEM((n, rows, 2 * GW), BF16),
            pltpu.VMEM((GROUP, rows, GW), BF16),
            pltpu.VMEM((GROUP, rows, GW), BF16),
            pltpu.VMEM((GROUP, rows, GW), BF16),
            pltpu.VMEM((GROUP, rows, dm), BF16),
            pltpu.VMEM((owners, own_rows, dm), F32),
            pltpu.VMEM((owners, own_rows, dm), BF16),
            pltpu.VMEM((cols, own_rows, dm), BF16),
            pltpu.VMEM((2 * n, own_rows, dm // 2), BF16),
            dma((GROUP,)), dma((GROUP,)),
            dma((GROUP,)), dma((GROUP,)),
            dma((GROUP,)), dma((GROUP,)),
            dma((GROUP,)), dma((GROUP,)),
            dma((2, cols, GROUP)), dma((cols, GROUP)),
            dma((cols,)), dma((cols,)),
            dma((6, cols)), dma((5, cols)),
        ],
        compiler_params=pltpu.CompilerParams(
            collective_id=1, has_side_effects=True, vmem_limit_bytes=52 * 2**20
        ),
        name="attend",
    )(tok, kv, q, cotangent, output_weight)

    output_grad = (
        grad.reshape(cols, GROUP, 2, own_rows, dm // 2)[:owners]
        .transpose(1, 0, 3, 2, 4)
        .reshape(dm, dm)
        .astype(F32)
    )
    return mixed, output_grad


def solution(mesh):
    part = P(("slide", "tile"))
    in_specs = (part, part) + (P(),) * 6 + (part,)
    out_specs = (part, P("slide"))
    return jax.shard_map(
        functools.partial(local, mesh.shape["tile"]),
        mesh=mesh, in_specs=in_specs, out_specs=out_specs, check_vma=False,
    )
```

time: 402 us -> 106 us (0.26)
  waiting for transfers between devices: 311 us -> 0 us
  Pallas kernels: 0 us -> 96.5 us
  local copies, waits for them, and re-layouts: 42.8 us -> 7.12 us
  matrix products: 26.5 us -> 0 us
  between operations: 14.1 us -> 0.73 us
  other arithmetic: 7.32 us -> 1.53 us
    all_gather x3 -> x0, waiting for transfers between devices: 182 us -> none  [the longest x1 63.9 us: local(): lax.all_gather(keys, 'tile', axis=0, tiled=True).reshape(-1, HEADS, HD)]
    psum x1 -> x0, waiting for transfers between devices: 129 us -> none  [local(): output_grad = lax.psum(grad_term, 'tile')]
    pallas_call x0 -> x2, Pallas kernels: none -> 96.5 us  [the longest x1 62.8 us: local(): pl.pallas_call(functools.partial(attend_kernel, cols, own_rows), out_shap...]
    dot_general x17 -> x0, matrix products: 26.5 us -> none  [the longest x1 7.94 us: local(): jnp.einsum('hqk,khd->hqd', weights.astype(jnp.bfloat16), value_heads, pre...]
    gather x8 -> x0, local copies, waits for them, and re-layouts: 14.6 us -> none  [the longest x1 2.16 us: pad_tiles(): right_col = all_faces[links[:, 4], 2]]
    all_gather x2 -> x0, local copies, waits for them, and re-layouts: 9.42 us -> none  [the longest x1 4.71 us: local(): lax.all_gather(values, 'tile', axis=0, tiled=True).reshape(-1, HEADS, HD)]
    concatenate x3 -> x0, other arithmetic: 4.16 us -> none  [the longest x1 1.7 us: pad_tiles(): jnp.concatenate([top_row[:, None], middle, bottom_row[:, None]], axis=1)]
    unnamed x17 -> x7, local copies, waits for them, and re-layouts: 8.31 us -> 4.55 us
  transfers between devices with their start and end apart: 4 -> 0, of which waited for: 4 -> 0; matrix products, arithmetic and copies ran while one was open for 4% -> 0% of each run, Pallas kernels for 0% -> 0%
where the time goes in v1:
time: 106 us
  Pallas kernels  96.5 us (91%)
  local copies, waits for them, and re-layouts  7.12 us (7%)
  other arithmetic  1.53 us (1%)
    pallas_call x1, Pallas kernels, local(): pl.pallas_call(functools.partial(attend_kernel, cols, own_rows), out_shap...  62.8 us
    pallas_call x1, Pallas kernels, local(): pl.pallas_call(functools.partial(embed_kernel, cols), out_shape=(jax.Shap...  33.7 us
    unnamed x7, local copies, waits for them, and re-layouts  4.55 us

profile of v1, /device:TPU:0, one launch (start us, length us, event | category | flops | bytes accessed | tf_op | source)
XLA Modules:
  0.0 105.9 jit_solution(12798074317583701339)
XLA Ops:
  0.6 2.3 %copy.22 = bf16[2,32,32,256]{3,0,2,1:T(2,128)(2,1)S(1)} copy(bf16[2,32,32,256]{3,2,1,0:T(8,128)(2,1)} %param.9) | data formatting | bytes 2097152 | tf_op args[0]
  3.1 0.0 copy-start.1
  3.1 1.2 %copy.23 = bf16[4,4,2,8,8,256]{5,4,3,2,1,0:T(8,128)(2,1)} copy(bf16[4,4,2,8,8,256]{5,2,1,4,0,3:T(2,128)(2,1)S(1)} %bitcast.39) | data formatting | bytes 2097152 | tf_op jit(solution)/shard_map/transpose | solution.py:410
  4.4 0.0 copy-done.1
  4.4 0.0 copy-start
  4.4 33.7 %embed.1 = (bf16[128,768]{1,0:T(8,128)(2,1)S(1)}, bf16[4,128,384]{2,1,0:T(8,128)(2,1)S(1)}, bf16[4,128,192]{2,1,0:T(8,128)(2,1)S(1)}) custom-call(bf16[4,4,128,256]{3,2,1,0:T(8,128)(2,1)} %bitcast.40, bf16[2,4,32,256]{3,2,1,0:T(8,128)(2,1)S(1)} %pad_maximum_fusion.own_ref, s32[2,8]{1,0:T(2,128)S(1)} %copy-done.1, bf16[9,256,256]{2,1,0:T(8,128)(2,1)} %bitcast.42, ...), custom_call_target="tpu_custom_call" | custom-call | tf_op jit(solution)/shard_map/embed/pallas_call | solution.py:422
  38.1 0.0 copy-done
  38.1 62.8 %attend.1 = (bf16[128,768]{1,0:T(8,128)(2,1)S(1)}, bf16[32,48,384]{2,1,0:T(8,128)(2,1)}) custom-call(bf16[128,768]{1,0:T(8,128)(2,1)S(1)} %get-tuple-element.7.tok_ref, bf16[4,128,384]{2,1,0:T(8,128)(2,1)S(1)} %get-tuple-element.8.kv_ref, bf16[4,128,192]{2,1,0:T(8,128)(2,1)S(1)} %get-tuple-element.9.q_ref, bf16[128,768]{1,0:T(8,128)(2,1)S(1)} %copy-done, ...), custom_call_target="tpu_custom_call" | custom-call | tf_op jit(solution)/shard_map/attend/pallas_call | solution.py:451
  100.9 1.5 %convert_bitcast_fusion = f32[4,4,48,2,384]{4,2,3,0,1:T(8,128)S(1)} fusion(bf16[4,4,2,48,384]{4,3,2,1,0:T(8,128)(2,1)} %bitcast.43), kind=kLoop, calls=%fused_computation | loop fusion | flops 589824 | bytes 3538944 | tf_op jit(solution)/shard_map/convert_element_type | solution.py:487
  102.5 1.2 %copy.32 = f32[4,4,48,2,384]{4,3,2,1,0:T(2,128)S(1)} copy(f32[4,4,48,2,384]{4,2,3,0,1:T(8,128)S(1)} %convert_bitcast_fusion) | data formatting | bytes 4718592 | tf_op jit(solution)/shard_map/convert_element_type | solution.py:487
  103.7 1.6 %copy.37 = f32[96,8,2,384]{3,1,2,0:T(8,128)} copy(f32[96,8,2,384]{3,2,1,0:T(2,128)S(1)} %bitcast.36) | data formatting | bytes 4718592
  105.2 0.7 copy.43
  (5 shorter events, 0.1 us)
Async XLA Ops:
  3.1 1.3 %copy-start.1 = (s32[2,8]{1,0:T(2,128)S(1)}, s32[2,8]{1,0:T(2,128)}, u32[]{:S(2)}) copy-start(s32[2,8]{1,0:T(2,128)} %nb_ref.1) | copy-start | bytes 196
  4.4 33.7 %copy-start = (bf16[128,768]{1,0:T(8,128)(2,1)S(1)}, bf16[128,768]{1,0:T(8,128)(2,1)}, u32[]{:S(2)}) copy-start(bf16[128,768]{1,0:T(8,128)(2,1)} %cot_ref.1) | copy-start | bytes 589828

commit v2 on v1

--- a/solution.py
+++ b/solution.py
@@ -55,31 +55,25 @@
     return [(c - s, c - s >= 0, True, False), (c + s, c + s < cols, False, True)]
 
 
-def gather_all(buf, cols, ss, rs):
+def gather_steps(full, half, cols, ss, rs):
     me, c, p = place()
     px, py, pd = plane_partners(p)
 
-    def full(k, q):
-        return buf.at[pl.ds(2 * (k * GROUP + q), 2)]
-
-    def half(k, q, h):
-        return buf.at[2 * (k * GROUP + q) + h]
-
     def z_copy(k, d):
         to = c + 1 - 2 * d
-        return remote(full(k, p), full(k, p), ss.at[d, k], rs.at[0, k], to * GROUP + p)
+        return remote(full(k, p), full(k, p), ss(d, k), rs(0, k), to * GROUP + p)
 
     def x_copy(k, q):
-        return remote(full(k, q), full(k, q), ss.at[2, k], rs.at[1, k], c * GROUP + px)
+        return remote(full(k, q), full(k, q), ss(2, k), rs(1, k), c * GROUP + px)
 
     def y_copy(k, q):
-        return remote(full(k, q), full(k, q), ss.at[3, k], rs.at[2, k], c * GROUP + py)
+        return remote(full(k, q), full(k, q), ss(3, k), rs(2, k), c * GROUP + py)
 
     def y_pass(k, q):
-        return remote(half(k, q, 0), half(k, q, 0), ss.at[4, k], rs.at[3, k], c * GROUP + py)
+        return remote(half(k, q, 0), half(k, q, 0), ss(4, k), rs(3, k), c * GROUP + py)
 
     def x_pass(k, q):
-        return remote(half(k, q, 1), half(k, q, 1), ss.at[5, k], rs.at[4, k], c * GROUP + px)
+        return remote(half(k, q, 1), half(k, q, 1), ss(5, k), rs(4, k), c * GROUP + px)
 
     def pass_on(s):
         for k, ok, _, _ in stage_blocks(c, cols, s):
@@ -105,7 +99,9 @@
             when(ok, body)
         if s > 0:
             pass_on(s - 1)
+        yield
     pass_on(cols - 1)
+    yield
     for k in range(cols):
         y_pass(k, pd).wait_recv()
         x_pass(k, pd).wait_recv()
@@ -122,6 +118,16 @@
                 y_pass(k, px).wait_send()
                 x_pass(k, py).wait_send()
             when(ok, body)
+
+
+def advance(steps):
+    return next(steps, "end") != "end"
+
+
+def drain(*many):
+    live = list(many)
+    while live:
+        live = [steps for steps in live if advance(steps)]
 
 
 def embed_kernel(
@@ -165,7 +171,11 @@
     def _():
         pl.semaphore_wait(barrier, 3)
 
-    gather_all(faces, cols, ss, rs)
+    drain(gather_steps(
+        lambda k, q: faces.at[pl.ds(2 * (k * GROUP + q), 2)],
+        lambda k, q, h: faces.at[2 * (k * GROUP + q) + h],
+        cols, lambda i, k: ss.at[i, k], lambda i, k: rs.at[i, k],
+    ))
 
     loads[0].wait()
     ch = ep.shape[3]
@@ -232,7 +242,9 @@
     for g in range(GROUP):
         part = slice(g * GW, (g + 1) * GW)
         q_ref[g] = query[:, part].astype(BF16)
-        kv_ref[g] = jnp.concatenate([keys[:, part], values[:, part]], axis=1).astype(BF16)
+        for h in range(GH):
+            part = slice(g * GW + h * HD, g * GW + h * HD + HD)
+            kv_ref[g, h] = jnp.concatenate([keys[:, part], values[:, part]], axis=1).astype(BF16)
 
 
 def attend_kernel(
@@ -242,7 +254,7 @@
     kv_ss, kv_rs, q_ss, q_rs, c_ss, c_rs, o_ss, o_rs, z_ss, z_rs, p_ss, p_rs, ss, rs,
 ):
     n = cols * GROUP
-    owners = GW // own_rows
+    owners = HD // own_rows
     me, c, p = place()
     barrier = pltpu.get_barrier_semaphore()
     for d in range(1, GROUP):
@@ -253,14 +265,17 @@
         pl.semaphore_signal(
             barrier, inc=1, device_id={"tile": (c + d) % cols * GROUP + p}, device_id_type=MESH
         )
-    kvg[me] = kv_ref[p]
+    for h in range(GH):
+        kvg[h, me] = kv_ref[p, h]
     qg[p] = q_ref[p]
     cotg[p] = cot_ref[...]
     pl.semaphore_wait(barrier, GROUP - 1 + cols - 1)
 
-    def kv_plane(d):
+    def kv_plane(h, d):
         g = (p + d) % GROUP
-        return remote(kv_ref.at[g], kvg.at[me], kv_ss.at[d], kv_rs.at[d], c * GROUP + g)
+        return remote(
+            kv_ref.at[g, h], kvg.at[h, me], kv_ss.at[h, d], kv_rs.at[h, d], c * GROUP + g
+        )
 
     def q_plane(d):
         g = (p + d) % GROUP
@@ -270,47 +285,40 @@
         g = (p + d) % GROUP
         return remote(cotg.at[p], cotg.at[p], c_ss.at[d], c_rs.at[d], c * GROUP + g)
 
-    def z_copy(k, d, way):
-        b = k * GROUP + (p + GROUP - d) % GROUP
+    def o_plane(d):
+        g = (p + d) % GROUP
+        return remote(og.at[g], ogr.at[p], o_ss.at[d], o_rs.at[d], c * GROUP + g)
+
+    def z_copy(h, k, way):
+        block = kvg.at[h, pl.ds(k * GROUP, GROUP)]
         to = c + 1 - 2 * way
-        return remote(kvg.at[b], kvg.at[b], z_ss.at[way, k, d], z_rs.at[k, d], to * GROUP + p)
-
-    for d in range(1, GROUP):
-        kv_plane(d).start()
-    for d in range(1, GROUP):
-        q_plane(d).start()
-    for s in range(cols):
-        for d in range(GROUP):
+        return remote(block, block, z_ss.at[h, way, k], z_rs.at[h, k], to * GROUP + p)
+
+    def z_steps(h):
+        for d in range(1, GROUP):
+            kv_plane(h, d).wait_recv()
+        for s in range(cols):
             for k, ok, up, down in stage_blocks(c, cols, s):
                 def body(k=k, up=up, down=down):
                     if s > 0:
-                        z_copy(k, d, 0).wait_recv()
-                    elif d > 0:
-                        kv_plane(d).wait_recv()
+                        z_copy(h, k, 0).wait_recv()
                     if s < cols - 1:
                         if up:
-                            when(c + 1 < cols, lambda: z_copy(k, d, 0).start())
+                            when(c + 1 < cols, lambda: z_copy(h, k, 0).start())
                         if down:
-                            when(c >= 1, lambda: z_copy(k, d, 1).start())
+                            when(c >= 1, lambda: z_copy(h, k, 1).start())
                 when(ok, body)
-        if s == 0:
-            for d in range(1, GROUP):
-                c_plane(d).start()
-    for d in range(1, GROUP):
-        q_plane(d).wait_recv()
+            yield
 
     factor = HD ** (-0.5) * math.log2(math.e)
 
-    def o_plane(d):
-        g = (p + d) % GROUP
-        return remote(og.at[g], ogr.at[p], o_ss.at[d], o_rs.at[d], c * GROUP + g)
-
-    def attend(i, carry):
-        g = (p + 1 + i) % GROUP
-        for h in range(GH):
-            lanes = slice(h * HD, (h + 1) * HD)
-            key = kvg[:, :, lanes].reshape(n * 128, HD)
-            value = kvg[:, :, GW + h * HD:GW + (h + 1) * HD].reshape(n * 128, HD)
+    def attend(h, first, last):
+        lanes = slice(h * HD, (h + 1) * HD)
+
+        def block(i, carry):
+            g = (p + 1 + i) % GROUP
+            key = kvg[h, :, :, 0:HD].reshape(n * 128, HD)
+            value = kvg[h, :, :, HD:2 * HD].reshape(n * 128, HD)
             query = qg[g, :, lanes]
             scores = lax.dot_general(
                 query, key, (((1,), (1,)), ((), ())), preferred_element_type=F32
@@ -320,30 +328,97 @@
             total = jnp.sum(weights, axis=1, keepdims=True)
             out = jnp.dot(weights.astype(BF16), value, preferred_element_type=F32)
             og[g, :, lanes] = (out / total).astype(BF16)
-
-        return carry
-
-    lax.fori_loop(0, GROUP, attend, 0)
-    for d in range(1, GROUP):
-        o_plane(d).start()
-    for d in range(1, GROUP):
-        c_plane(d).wait_recv()
-    part = lax.dot_general(
-        og[...].reshape(GROUP * 128, GW), cotg[...].reshape(GROUP * 128, -1),
-        (((0,), (0,)), ((), ())), preferred_element_type=F32,
-    )
-    part_f[...] = part.reshape(part_f.shape)
-    part_s[...] = part.reshape(part_f.shape).astype(BF16)
-
-    def p_copy(d):
+            return carry
+
+        lax.fori_loop(first, last, block, 0)
+
+    def p_copy(h, d):
         j = (c + d) % cols
         return j, remote(
-            part_s.at[j], part_r.at[d], p_ss.at[d], p_rs.at[d], j * GROUP + p
-        )
-
-    for d in range(1, cols):
-        j, copy = p_copy(d)
-        when(j < owners if owners < cols else True, copy.start)
+            part_s.at[h, j], part_r.at[h, d], p_ss.at[h, d], p_rs.at[h, d], j * GROUP + p
+        )
+
+    def grad_steps(h):
+        part = lax.dot_general(
+            og[:, :, h * HD:(h + 1) * HD].reshape(GROUP * 128, HD),
+            cotg[...].reshape(GROUP * 128, -1),
+            (((0,), (0,)), ((), ())), preferred_element_type=F32,
+        ).reshape(owners, own_rows, -1)
+        part_f[h] = part
+        part_s[h] = part.astype(BF16)
+        for d in range(1, cols):
+            j, copy = p_copy(h, d)
+            when(j < owners if owners < cols else True, copy.start)
+        yield
+
+        def reduce():
+            acc = part_f[h, c]
+            for d in range(1, cols):
+                p_copy(h, d)[1].wait_recv()
+                acc = acc + part_r[h, d].astype(F32)
+            gr[h, me] = acc.astype(BF16)
+
+        def nothing():
+            gr[h, me] = jnp.zeros(gr.shape[2:], BF16)
+
+        if owners < cols:
+            pl.when(c < owners)(reduce)
+            pl.when(c >= owners)(nothing)
+        else:
+            reduce()
+        wide = gr.shape[3] // 2
+        yield from gather_steps(
+            lambda k, q: gr.at[h, k * GROUP + q],
+            lambda k, q, i: gr.at[h, k * GROUP + q, :, pl.ds(i * wide, wide)],
+            cols, lambda i, k: ss.at[h, i, k], lambda i, k: rs.at[h, i, k],
+        )
+        for d in range(1, cols):
+            j, copy = p_copy(h, d)
+            when(j < owners if owners < cols else True, copy.wait_send)
+
+    for h in range(GH):
+        for d in range(1, GROUP):
+            kv_plane(h, d).start()
+        if h == 0:
+            for d in range(1, GROUP):
+                q_plane(d).start()
+    for d in range(1, GROUP):
+        c_plane(d).start()
+    z = [z_steps(h) for h in range(GH)]
+    grads = [grad_steps(h) for h in range(GH)]
+    advance(z[0])
+    advance(z[1])
+    advance(z[0])
+    advance(z[2])
+    advance(z[0])
+    advance(z[1])
+    drain(z[0])
+    for d in range(1, GROUP):
+        q_plane(d).wait_recv()
+    attend(0, 0, 2)
+    advance(z[1])
+    advance(z[2])
+    attend(0, 2, 4)
+    drain(z[1])
+    advance(z[2])
+    for d in range(1, GROUP):
+        c_plane(d).wait_recv()
+    advance(grads[0])
+    attend(1, 0, 2)
+    drain(z[2])
+    advance(grads[0])
+    attend(1, 2, 4)
+    advance(grads[0])
+    advance(grads[1])
+    attend(2, 0, 2)
+    advance(grads[0])
+    advance(grads[1])
+    attend(2, 2, 4)
+    for d in range(1, GROUP):
+        o_plane(d).start()
+    advance(grads[2])
+    advance(grads[0])
+    advance(grads[1])
     ogr[p] = og[p]
     for d in range(1, GROUP):
         o_plane(d).wait_recv()
@@ -353,44 +428,27 @@
             ogr[g], wo_ref[g * GW:(g + 1) * GW], preferred_element_type=F32
         )
     mixed_ref[...] = total.astype(BF16)
-
-    def reduce():
-        acc = part_f[c]
-        for d in range(1, cols):
-            p_copy(d)[1].wait_recv()
-            acc = acc + part_r[d].astype(F32)
-        wide = acc.shape[1] // 2
-        gr[2 * me] = acc[:, :wide].astype(BF16)
-        gr[2 * me + 1] = acc[:, wide:].astype(BF16)
-
-    def nothing():
-        gr[2 * me] = jnp.zeros(gr.shape[1:], BF16)
-        gr[2 * me + 1] = jnp.zeros(gr.shape[1:], BF16)
-
-    if owners < cols:
-        pl.when(c < owners)(reduce)
-        pl.when(c >= owners)(nothing)
-    else:
-        reduce()
-    gather_all(gr, cols, ss, rs)
-    grad_ref[...] = gr[...]
-
-    for d in range(1, GROUP):
-        kv_plane(d).wait_send()
+    drain(*grads)
+    for q in range(GROUP):
+        for h in range(GH):
+            for k in range(owners):
+                row = q * GW + h * HD + k * own_rows
+                grad_ref[row:row + own_rows] = gr[h, k * GROUP + q]
+
+    for d in range(1, GROUP):
+        for h in range(GH):
+            kv_plane(h, d).wait_send()
         q_plane(d).wait_send()
         c_plane(d).wait_send()
         o_plane(d).wait_send()
-    for d in range(1, cols):
-        j, copy = p_copy(d)
-        when(j < owners if owners < cols else True, copy.wait_send)
-    for s in range(cols - 1):
-        for d in range(GROUP):
+    for h in range(GH):
+        for s in range(cols - 1):
             for k, ok, up, down in stage_blocks(c, cols, s):
                 def body(k=k, up=up, down=down):
                     if up:
-                        when(c + 1 < cols, lambda: z_copy(k, d, 0).wait_send())
+                        when(c + 1 < cols, lambda: z_copy(h, k, 0).wait_send())
                     if down:
-                        when(c >= 1, lambda: z_copy(k, d, 1).wait_send())
+                        when(c >= 1, lambda: z_copy(h, k, 1).wait_send())
                 when(ok, body)
 
 
@@ -423,7 +481,7 @@
         functools.partial(embed_kernel, cols),
         out_shape=(
             jax.ShapeDtypeStruct((rows, dm), BF16),
-            jax.ShapeDtypeStruct((GROUP, rows, 2 * GW), BF16),
+            jax.ShapeDtypeStruct((GROUP, GH, rows, 2 * HD), BF16),
             jax.ShapeDtypeStruct((GROUP, rows, GW), BF16),
         ),
         in_specs=[anyw, vmem, pl.BlockSpec(memory_space=pltpu.SMEM), vmem, anyw, anyw, anyw, anyw],
@@ -446,47 +504,40 @@
         query_weight, key_weight, value_weight,
     )
 
-    own_rows = max(16, GW // cols // 16 * 16)
-    owners = GW // own_rows
+    own_rows = max(16, HD // cols // 16 * 16)
+    owners = HD // own_rows
     mixed, grad = pl.pallas_call(
         functools.partial(attend_kernel, cols, own_rows),
         out_shape=(
             jax.ShapeDtypeStruct((rows, dm), BF16),
-            jax.ShapeDtypeStruct((2 * n, own_rows, dm // 2), BF16),
+            jax.ShapeDtypeStruct((dm, dm), BF16),
         ),
         in_specs=[vmem] * 5,
         out_specs=(vmem, vmem),
         scratch_shapes=[
-            pltpu.VMEM((n, rows, 2 * GW), BF16),
+            pltpu.VMEM((GH, n, rows, 2 * HD), BF16),
             pltpu.VMEM((GROUP, rows, GW), BF16),
             pltpu.VMEM((GROUP, rows, GW), BF16),
             pltpu.VMEM((GROUP, rows, GW), BF16),
             pltpu.VMEM((GROUP, rows, dm), BF16),
-            pltpu.VMEM((owners, own_rows, dm), F32),
-            pltpu.VMEM((owners, own_rows, dm), BF16),
-            pltpu.VMEM((cols, own_rows, dm), BF16),
-            pltpu.VMEM((2 * n, own_rows, dm // 2), BF16),
+            pltpu.VMEM((GH, owners, own_rows, dm), F32),
+            pltpu.VMEM((GH, owners, own_rows, dm), BF16),
+            pltpu.VMEM((GH, cols, own_rows, dm), BF16),
+            pltpu.VMEM((GH, n, own_rows, dm), BF16),
+            dma((GH, GROUP)), dma((GH, GROUP)),
             dma((GROUP,)), dma((GROUP,)),
             dma((GROUP,)), dma((GROUP,)),
             dma((GROUP,)), dma((GROUP,)),
-            dma((GROUP,)), dma((GROUP,)),
-            dma((2, cols, GROUP)), dma((cols, GROUP)),
-            dma((cols,)), dma((cols,)),
-            dma((6, cols)), dma((5, cols)),
+            dma((GH, 2, cols)), dma((GH, cols)),
+            dma((GH, cols)), dma((GH, cols)),
+            dma((GH, 6, cols)), dma((GH, 5, cols)),
         ],
         compiler_params=pltpu.CompilerParams(
             collective_id=1, has_side_effects=True, vmem_limit_bytes=52 * 2**20
         ),
         name="attend",
     )(tok, kv, q, cotangent, output_weight)
-
-    output_grad = (
-        grad.reshape(cols, GROUP, 2, own_rows, dm // 2)[:owners]
-        .transpose(1, 0, 3, 2, 4)
-        .reshape(dm, dm)
-        .astype(F32)
-    )
-    return mixed, output_grad
+    return mixed, grad.astype(F32)
 
 
 def solution(mesh):

time: 106 us -> 109 us (1.028)
  Pallas kernels: 96.5 us -> 101 us
  local copies, waits for them, and re-layouts: 7.12 us -> 4.34 us
  other arithmetic: 1.53 us -> 2.87 us
    pallas_call x1, Pallas kernels: 62.8 us -> 67.2 us  [local(): pl.pallas_call(functools.partial(attend_kernel, cols, own_rows), out_shap...]
    unnamed x7 -> x6, local copies, waits for them, and re-layouts: 4.55 us -> 3 us
    convert_element_type x1, other arithmetic: 1.51 us -> 2.85 us  [local(): return (mixed, grad.astype(F32))]
    convert_element_type x1 -> x0, local copies, waits for them, and re-layouts: 1.21 us -> none  [local(): output_grad = grad.reshape(cols, GROUP, 2, own_rows, dm // 2)[:owners].tr...]
where the time goes in v2:
time: 109 us
  Pallas kernels  101 us (93%)
  local copies, waits for them, and re-layouts  4.34 us (4%)
  other arithmetic  2.87 us (3%)
    pallas_call x1, Pallas kernels, local(): pl.pallas_call(functools.partial(attend_kernel, cols, own_rows), out_shap...  67.2 us
    pallas_call x1, Pallas kernels, local(): pl.pallas_call(functools.partial(embed_kernel, cols), out_shape=(jax.Shap...  33.7 us
    unnamed x6, local copies, waits for them, and re-layouts  3 us
    convert_element_type x1, other arithmetic, local(): return (mixed, grad.astype(F32))  2.85 us

profile of v2, /device:TPU:0, one launch (start us, length us, event | category | flops | bytes accessed | tf_op | source)
XLA Modules:
  0.0 108.8 jit_solution(14404152341790858840)
XLA Ops:
  0.6 2.3 %copy.20 = bf16[2,32,32,256]{3,0,2,1:T(2,128)(2,1)S(1)} copy(bf16[2,32,32,256]{3,2,1,0:T(8,128)(2,1)} %param.9) | data formatting | bytes 2097152 | tf_op args[0]
  3.1 0.0 copy-start.1
  3.1 1.2 %copy.21 = bf16[4,4,2,8,8,256]{5,4,3,2,1,0:T(8,128)(2,1)} copy(bf16[4,4,2,8,8,256]{5,2,1,4,0,3:T(2,128)(2,1)S(1)} %bitcast.31) | data formatting | bytes 2097152 | tf_op jit(solution)/shard_map/transpose | solution.py:468
  4.4 0.0 copy-done.1
  4.4 0.0 copy-start
  4.4 33.7 %embed.1 = (bf16[128,768]{1,0:T(8,128)(2,1)S(1)}, bf16[4,3,128,128]{3,2,1,0:T(8,128)(2,1)S(1)}, bf16[4,128,192]{2,1,0:T(8,128)(2,1)S(1)}) custom-call(bf16[4,4,128,256]{3,2,1,0:T(8,128)(2,1)} %bitcast.32, bf16[2,4,32,256]{3,2,1,0:T(8,128)(2,1)S(1)} %pad_maximum_fusion.own_ref, s32[2,8]{1,0:T(2,128)S(1)} %copy-done.1, bf16[9,256,256]{2,1,0:T(8,128)(2,1)} %bitcast.33, ...), custom_call_target="tpu_custom_call" | custom-call | tf_op jit(solution)/shard_map/embed/pallas_call | solution.py:480
  38.1 0.0 copy-done
  38.1 67.2 %attend.1 = (bf16[128,768]{1,0:T(8,128)(2,1)S(1)}, bf16[768,768]{1,0:T(8,128)(2,1)}) custom-call(bf16[128,768]{1,0:T(8,128)(2,1)S(1)} %get-tuple-element.7.tok_ref, bf16[4,3,128,128]{3,2,1,0:T(8,128)(2,1)S(1)} %get-tuple-element.8.kv_ref, bf16[4,128,192]{2,1,0:T(8,128)(2,1)S(1)} %get-tuple-element.9.q_ref, bf16[128,768]{1,0:T(8,128)(2,1)S(1)} %copy-done, ...), custom_call_target="tpu_custom_call" | custom-call | tf_op jit(solution)/shard_map/attend/pallas_call | solution.py:509
  105.3 2.8 %convert_element_type.3 = f32[768,768]{1,0:T(8,128)} convert(bf16[768,768]{1,0:T(8,128)(2,1)} %get-tuple-element.11) | non-fusion elementwise | flops 589824 | bytes 3538944 | tf_op jit(solution)/shard_map/convert_element_type | solution.py:540
  108.1 0.7 copy.39
  (5 shorter events, 0.1 us)
Async XLA Ops:
  3.1 1.3 %copy-start.1 = (s32[2,8]{1,0:T(2,128)S(1)}, s32[2,8]{1,0:T(2,128)}, u32[]{:S(2)}) copy-start(s32[2,8]{1,0:T(2,128)} %nb_ref.1) | copy-start | bytes 196
  4.4 33.7 %copy-start = (bf16[128,768]{1,0:T(8,128)(2,1)S(1)}, bf16[128,768]{1,0:T(8,128)(2,1)}, u32[]{:S(2)}) copy-start(bf16[128,768]{1,0:T(8,128)(2,1)} %cot_ref.1) | copy-start | bytes 589828

commit v3 on v2

--- a/solution.py
+++ b/solution.py
@@ -120,6 +120,37 @@
             when(ok, body)
 
 
+def direct_steps(full, cols, zs, zr, ps, pr):
+    me, c, p = place()
+
+    def z_copy(d, k):
+        to = (c + d) % cols
+        return remote(full(k, p), full(k, p), zs(d), zr(d), to * GROUP + p)
+
+    def plane(d, e, q):
+        k = (c + cols - d) % cols
+        return remote(full(k, q), full(k, q), ps(d, e), pr(d, e), c * GROUP + (p + e) % GROUP)
+
+    for d in range(1, cols):
+        z_copy(d, c).start()
+    for e in range(1, GROUP):
+        plane(0, e, p).start()
+    yield
+    for d in range(1, cols):
+        z_copy(d, (c + cols - d) % cols).wait_recv()
+        for e in range(1, GROUP):
+            plane(d, e, p).start()
+    yield
+    for d in range(cols):
+        for e in range(1, GROUP):
+            plane(d, e, (p + GROUP - e) % GROUP).wait_recv()
+    for d in range(cols):
+        if d:
+            z_copy(d, c).wait_send()
+        for e in range(1, GROUP):
+            plane(d, e, p).wait_send()
+
+
 def advance(steps):
     return next(steps, "end") != "end"
 
@@ -251,7 +282,7 @@
     cols, own_rows, tok_ref, kv_ref, q_ref, cot_ref, wo_ref,
     mixed_ref, grad_ref,
     kvg, qg, og, ogr, cotg, part_f, part_s, part_r, gr,
-    kv_ss, kv_rs, q_ss, q_rs, c_ss, c_rs, o_ss, o_rs, z_ss, z_rs, p_ss, p_rs, ss, rs,
+    kv_ss, kv_rs, q_ss, q_rs, c_ss, c_rs, o_ss, o_rs, z_ss, z_rs, p_ss, p_rs, zs, zr, ss, rs,
 ):
     n = cols * GROUP
     owners = HD // own_rows
@@ -314,23 +345,19 @@
 
     def attend(h, first, last):
         lanes = slice(h * HD, (h + 1) * HD)
-
-        def block(i, carry):
-            g = (p + 1 + i) % GROUP
-            key = kvg[h, :, :, 0:HD].reshape(n * 128, HD)
-            value = kvg[h, :, :, HD:2 * HD].reshape(n * 128, HD)
-            query = qg[g, :, lanes]
-            scores = lax.dot_general(
-                query, key, (((1,), (1,)), ((), ())), preferred_element_type=F32
-            )
-            top = jnp.max(scores, axis=1, keepdims=True)
-            weights = jnp.exp2((scores - top) * factor)
-            total = jnp.sum(weights, axis=1, keepdims=True)
-            out = jnp.dot(weights.astype(BF16), value, preferred_element_type=F32)
-            og[g, :, lanes] = (out / total).astype(BF16)
-            return carry
-
-        lax.fori_loop(first, last, block, 0)
+        count = (last - first) * 128
+        both = kvg[h].reshape(n * 128, 2 * HD)
+        query = qg[first:last, :, lanes].reshape(count, HD)
+        query = jnp.concatenate([query, jnp.zeros_like(query)], axis=1)
+        scores = lax.dot_general(
+            query, both, (((1,), (1,)), ((), ())), preferred_element_type=F32
+        )
+        top = jnp.max(scores, axis=1, keepdims=True)
+        weights = jnp.exp2((scores - top) * factor)
+        total = jnp.sum(weights, axis=1, keepdims=True)
+        out = jnp.dot(weights.astype(BF16), both, preferred_element_type=F32)
+        out = (out / total)[:, HD:].astype(BF16)
+        og[first:last, :, lanes] = out.reshape(last - first, 128, HD)
 
     def p_copy(h, d):
         j = (c + d) % cols
@@ -366,11 +393,10 @@
             pl.when(c >= owners)(nothing)
         else:
             reduce()
-        wide = gr.shape[3] // 2
-        yield from gather_steps(
-            lambda k, q: gr.at[h, k * GROUP + q],
-            lambda k, q, i: gr.at[h, k * GROUP + q, :, pl.ds(i * wide, wide)],
-            cols, lambda i, k: ss.at[h, i, k], lambda i, k: rs.at[h, i, k],
+        yield from direct_steps(
+            lambda k, q: gr.at[h, k * GROUP + q], cols,
+            lambda d: zs.at[h, d], lambda d: zr.at[h, d],
+            lambda d, e: ss.at[h, d, e], lambda d, e: rs.at[h, d, e],
         )
         for d in range(1, cols):
             j, copy = p_copy(h, d)
@@ -411,13 +437,11 @@
     advance(grads[0])
     advance(grads[1])
     attend(2, 0, 2)
-    advance(grads[0])
     advance(grads[1])
     attend(2, 2, 4)
     for d in range(1, GROUP):
         o_plane(d).start()
     advance(grads[2])
-    advance(grads[0])
     advance(grads[1])
     ogr[p] = og[p]
     for d in range(1, GROUP):
@@ -428,12 +452,13 @@
             ogr[g], wo_ref[g * GW:(g + 1) * GW], preferred_element_type=F32
         )
     mixed_ref[...] = total.astype(BF16)
-    drain(*grads)
+    advance(grads[2])
+    drain(grads[0], grads[1], grads[2])
     for q in range(GROUP):
         for h in range(GH):
             for k in range(owners):
                 row = q * GW + h * HD + k * own_rows
-                grad_ref[row:row + own_rows] = gr[h, k * GROUP + q]
+                grad_ref[row:row + own_rows] = gr[h, k * GROUP + q].astype(F32)
 
     for d in range(1, GROUP):
         for h in range(GH):
@@ -510,7 +535,7 @@
         functools.partial(attend_kernel, cols, own_rows),
         out_shape=(
             jax.ShapeDtypeStruct((rows, dm), BF16),
-            jax.ShapeDtypeStruct((dm, dm), BF16),
+            jax.ShapeDtypeStruct((dm, dm), F32),
         ),
         in_specs=[vmem] * 5,
         out_specs=(vmem, vmem),
@@ -530,14 +555,15 @@
             dma((GROUP,)), dma((GROUP,)),
             dma((GH, 2, cols)), dma((GH, cols)),
             dma((GH, cols)), dma((GH, cols)),
-            dma((GH, 6, cols)), dma((GH, 5, cols)),
+            dma((GH, cols)), dma((GH, cols)),
+            dma((GH, cols, GROUP)), dma((GH, cols, GROUP)),
         ],
         compiler_params=pltpu.CompilerParams(
             collective_id=1, has_side_effects=True, vmem_limit_bytes=52 * 2**20
         ),
         name="attend",
     )(tok, kv, q, cotangent, output_weight)
-    return mixed, grad.astype(F32)
+    return mixed, grad
 
 
 def solution(mesh):

time: 109 us -> 105 us (0.963)
  Pallas kernels: 101 us -> 96.2 us
  local copies, waits for them, and re-layouts: 4.34 us -> 7.57 us
  other arithmetic: 2.87 us -> 0.02 us
    pallas_call x1, Pallas kernels: 67.2 us -> 62.5 us  [local(): pl.pallas_call(functools.partial(attend_kernel, cols, own_rows), out_shap...]
    unnamed x6 -> x7, local copies, waits for them, and re-layouts: 3 us -> 6.22 us
    convert_element_type x1 -> x0, other arithmetic: 2.85 us -> none  [local(): return (mixed, grad.astype(F32))]
where the time goes in v3:
time: 105 us
  Pallas kernels  96.2 us (92%)
  local copies, waits for them, and re-layouts  7.57 us (7%)
    pallas_call x1, Pallas kernels, local(): pl.pallas_call(functools.partial(attend_kernel, cols, own_rows), out_shap...  62.5 us
    pallas_call x1, Pallas kernels, local(): pl.pallas_call(functools.partial(embed_kernel, cols), out_shape=(jax.Shap...  33.7 us
    unnamed x7, local copies, waits for them, and re-layouts  6.22 us

profile of v3, /device:TPU:0, one launch (start us, length us, event | category | flops | bytes accessed | tf_op | source)
XLA Modules:
  0.0 104.5 jit_solution(10195372194993460239)
XLA Ops:
  0.6 2.3 %copy.20 = bf16[2,32,32,256]{3,0,2,1:T(2,128)(2,1)S(1)} copy(bf16[2,32,32,256]{3,2,1,0:T(8,128)(2,1)} %param.9) | data formatting | bytes 2097152 | tf_op args[0]
  3.1 0.0 copy-start.1
  3.1 1.2 %copy.21 = bf16[4,4,2,8,8,256]{5,4,3,2,1,0:T(8,128)(2,1)} copy(bf16[4,4,2,8,8,256]{5,2,1,4,0,3:T(2,128)(2,1)S(1)} %bitcast.31) | data formatting | bytes 2097152 | tf_op jit(solution)/shard_map/transpose | solution.py:493
  4.4 0.0 copy-done.1
  4.4 0.0 copy-start
  4.4 33.7 %embed.1 = (bf16[128,768]{1,0:T(8,128)(2,1)S(1)}, bf16[4,3,128,128]{3,2,1,0:T(8,128)(2,1)S(1)}, bf16[4,128,192]{2,1,0:T(8,128)(2,1)S(1)}) custom-call(bf16[4,4,128,256]{3,2,1,0:T(8,128)(2,1)} %bitcast.32, bf16[2,4,32,256]{3,2,1,0:T(8,128)(2,1)S(1)} %pad_maximum_fusion.own_ref, s32[2,8]{1,0:T(2,128)S(1)} %copy-done.1, bf16[9,256,256]{2,1,0:T(8,128)(2,1)} %bitcast.33, ...), custom_call_target="tpu_custom_call" | custom-call | tf_op jit(solution)/shard_map/embed/pallas_call | solution.py:505
  38.1 0.0 copy-done
  38.1 62.5 %attend.1 = (bf16[128,768]{1,0:T(8,128)(2,1)S(1)}, f32[768,768]{1,0:T(8,128)}) custom-call(bf16[128,768]{1,0:T(8,128)(2,1)S(1)} %get-tuple-element.5.tok_ref, bf16[4,3,128,128]{3,2,1,0:T(8,128)(2,1)S(1)} %get-tuple-element.6.kv_ref, bf16[4,128,192]{2,1,0:T(8,128)(2,1)S(1)} %get-tuple-element.7.q_ref, bf16[128,768]{1,0:T(8,128)(2,1)S(1)} %copy-done, ...), custom_call_target="tpu_custom_call" | custom-call | tf_op jit(solution)/shard_map/attend/pallas_call | solution.py:534
  100.6 0.7 copy.40
  101.3 3.2 %copy.41 = f32[768,768]{1,0:T(8,128)} copy(f32[768,768]{1,0:T(8,128)} %get-tuple-element.19) | data formatting | bytes 4718592
  (5 shorter events, 0.1 us)
Async XLA Ops:
  3.1 1.3 %copy-start.1 = (s32[2,8]{1,0:T(2,128)S(1)}, s32[2,8]{1,0:T(2,128)}, u32[]{:S(2)}) copy-start(s32[2,8]{1,0:T(2,128)} %nb_ref.1) | copy-start | bytes 196
  4.4 33.7 %copy-start = (bf16[128,768]{1,0:T(8,128)(2,1)S(1)}, bf16[128,768]{1,0:T(8,128)(2,1)}, u32[]{:S(2)}) copy-start(bf16[128,768]{1,0:T(8,128)(2,1)} %cot_ref.1) | copy-start | bytes 589828

commit v4 on v3

--- a/solution.py
+++ b/solution.py
@@ -35,12 +35,6 @@
     return me, me // GROUP, me % GROUP
 
 
-def plane_partners(p):
-    px = p + 1 - 2 * (p % 2)
-    py = p + 2 - 4 * (p // 2)
-    return px, py, GROUP - 1 - p
-
-
 def when(cond, body):
     if isinstance(cond, bool):
         if cond:
@@ -53,71 +47,6 @@
     if s == 0:
         return [(c, True, True, True)]
     return [(c - s, c - s >= 0, True, False), (c + s, c + s < cols, False, True)]
-
-
-def gather_steps(full, half, cols, ss, rs):
-    me, c, p = place()
-    px, py, pd = plane_partners(p)
-
-    def z_copy(k, d):
-        to = c + 1 - 2 * d
-        return remote(full(k, p), full(k, p), ss(d, k), rs(0, k), to * GROUP + p)
-
-    def x_copy(k, q):
-        return remote(full(k, q), full(k, q), ss(2, k), rs(1, k), c * GROUP + px)
-
-    def y_copy(k, q):
-        return remote(full(k, q), full(k, q), ss(3, k), rs(2, k), c * GROUP + py)
-
-    def y_pass(k, q):
-        return remote(half(k, q, 0), half(k, q, 0), ss(4, k), rs(3, k), c * GROUP + py)
-
-    def x_pass(k, q):
-        return remote(half(k, q, 1), half(k, q, 1), ss(5, k), rs(4, k), c * GROUP + px)
-
-    def pass_on(s):
-        for k, ok, _, _ in stage_blocks(c, cols, s):
-            def body(k=k):
-                x_copy(k, px).wait_recv()
-                y_pass(k, px).start()
-                y_copy(k, py).wait_recv()
-                x_pass(k, py).start()
-            when(ok, body)
-
-    for s in range(cols):
-        for k, ok, up, down in stage_blocks(c, cols, s):
-            def body(k=k, up=up, down=down):
-                if s > 0:
-                    z_copy(k, 0).wait_recv()
-                if s < cols - 1:
-                    if up:
-                        when(c + 1 < cols, lambda: z_copy(k, 0).start())
-                    if down:
-                        when(c >= 1, lambda: z_copy(k, 1).start())
-                x_copy(k, p).start()
-                y_copy(k, p).start()
-            when(ok, body)
-        if s > 0:
-            pass_on(s - 1)
-        yield
-    pass_on(cols - 1)
-    yield
-    for k in range(cols):
-        y_pass(k, pd).wait_recv()
-        x_pass(k, pd).wait_recv()
-    for s in range(cols):
-        for k, ok, up, down in stage_blocks(c, cols, s):
-            def body(k=k, up=up, down=down):
-                if s < cols - 1:
-                    if up:
-                        when(c + 1 < cols, lambda: z_copy(k, 0).wait_send())
-                    if down:
-                        when(c >= 1, lambda: z_copy(k, 1).wait_send())
-                x_copy(k, p).wait_send()
-                y_copy(k, p).wait_send()
-                y_pass(k, px).wait_send()
-                x_pass(k, py).wait_send()
-            when(ok, body)
 
 
 def direct_steps(full, cols, zs, zr, ps, pr):
@@ -164,11 +93,10 @@
 def embed_kernel(
     cols, x_ref, own_ref, nb_ref, cw_ref, pw_hbm, wq_hbm, wk_hbm, wv_hbm,
     tok_ref, kv_ref, q_ref,
-    faces, ep, pw, ww, ss, rs, local_sem,
+    faces, halo_s, halo_r, nb_all, nb_s, ep, pw, ww,
+    n_ss, n_rs, z_ss, z_rs, h_ss, h_rs, local_sem,
 ):
-    n = cols * GROUP
     me, c, p = place()
-    px, py, pd = plane_partners(p)
     loads = [
         pltpu.make_async_copy(x_ref, ep.at[pl.ds(1, 4), pl.ds(1, 4)], local_sem.at[0]),
         pltpu.make_async_copy(pw_hbm, pw, local_sem.at[1]),
@@ -176,11 +104,11 @@
         pltpu.make_async_copy(wk_hbm, ww.at[1], local_sem.at[3]),
         pltpu.make_async_copy(wv_hbm, ww.at[2], local_sem.at[4]),
     ]
-    for load in loads:
-        load.start()
     barrier = pltpu.get_barrier_semaphore()
-    pl.semaphore_signal(barrier, inc=1, device_id={"tile": c * GROUP + px}, device_id_type=MESH)
-    pl.semaphore_signal(barrier, inc=1, device_id={"tile": c * GROUP + py}, device_id_type=MESH)
+    for e in range(1, GROUP):
+        pl.semaphore_signal(
+            barrier, inc=1, device_id={"tile": c * GROUP + (p + e) % GROUP}, device_id_type=MESH
+        )
 
     @pl.when(c + 1 < cols)
     def _():
@@ -190,45 +118,101 @@
     def _():
         pl.semaphore_signal(barrier, inc=1, device_id={"tile": me - GROUP}, device_id_type=MESH)
 
-    faces[pl.ds(2 * me, 2)] = own_ref[...]
-    faces[2 * n] = jnp.zeros_like(faces[2 * n])
+    for load in loads:
+        load.start()
+    faces[pl.ds(2 * c, 2)] = own_ref[...]
+    faces[2 * cols] = jnp.zeros(faces.shape[1:], BF16)
+    nb_all[p] = nb_ref[...]
     inner = (c >= 1) & (c + 1 < cols)
 
     @pl.when(inner)
     def _():
-        pl.semaphore_wait(barrier, 4)
+        pl.semaphore_wait(barrier, GROUP + 1)
 
     @pl.when(jnp.logical_not(inner))
     def _():
-        pl.semaphore_wait(barrier, 3)
-
-    drain(gather_steps(
-        lambda k, q: faces.at[pl.ds(2 * (k * GROUP + q), 2)],
-        lambda k, q, h: faces.at[2 * (k * GROUP + q) + h],
-        cols, lambda i, k: ss.at[i, k], lambda i, k: rs.at[i, k],
-    ))
+        pl.semaphore_wait(barrier, GROUP)
+
+    def n_copy(e):
+        return remote(
+            nb_all.at[p], nb_all.at[p], n_ss.at[e], n_rs.at[e], c * GROUP + (p + e) % GROUP
+        )
+
+    def z_copy(k, way):
+        block = faces.at[pl.ds(2 * k, 2)]
+        to = c + 1 - 2 * way
+        return remote(block, block, z_ss.at[way, k], z_rs.at[k], to * GROUP + p)
+
+    def h_copy(e):
+        g = (p + e) % GROUP
+        return remote(halo_s.at[g], halo_r.at[p], h_ss.at[e], h_rs.at[e], c * GROUP + g)
+
+    for e in range(1, GROUP):
+        n_copy(e).start()
+    for s in range(cols):
+        for k, ok, up, down in stage_blocks(c, cols, s):
+            def body(k=k, up=up, down=down):
+                if s > 0:
+                    z_copy(k, 0).wait_recv()
+                if s < cols - 1:
+                    if up:
+                        when(c + 1 < cols, lambda: z_copy(k, 0).start())
+                    if down:
+                        when(c >= 1, lambda: z_copy(k, 1).start())
+            when(ok, body)
+        if s == 0:
+            for e in range(1, GROUP):
+                n_copy(e).wait_recv()
+            table = pltpu.make_async_copy(nb_all, nb_s, local_sem.at[5])
+            table.start()
+            table.wait()
+
+    side, ch = faces.shape[2], faces.shape[3]
+    tile_dev = 2 * GROUP
+
+    def fill(g, target):
+        for t in range(2):
+            def face(link, which):
+                index = nb_s[g, t, link]
+                found = faces[index // tile_dev * 2 + index % 2, which]
+                mine = index // 2 % GROUP == p
+                return jnp.where(mine, found.astype(F32), 0.0)
+
+            for at, (link, which) in enumerate(((1, 1), (6, 0), (3, 3), (4, 2))):
+                target[t, at * side:(at + 1) * side] = face(link, which).astype(BF16)
+            corners = jnp.concatenate(
+                [
+                    face(0, 1)[side - 1:side], face(2, 1)[0:1],
+                    face(5, 0)[side - 1:side], face(7, 0)[0:1],
+                    jnp.zeros((12, ch), F32),
+                ],
+                axis=0,
+            )
+            target[t, 4 * side:4 * side + 16] = corners.astype(BF16)
+
+    for e in range(1, GROUP):
+        g = (p + e) % GROUP
+        fill(g, halo_s.at[g])
+        h_copy(e).start()
+    fill(p, halo_r.at[p])
 
     loads[0].wait()
-    ch = ep.shape[3]
     first = lax.broadcasted_iota(jnp.int32, (64, ch), 0) % 8
 
     def spread(col):
         return jnp.broadcast_to(col[:, None, :], (8, 8, ch)).reshape(64, ch)
 
+    for e in range(1, GROUP):
+        h_copy(e).wait_recv()
     for t in range(2):
         rows = pl.ds(t * 64, 64)
-
-        def face(link, which):
-            return faces[nb_ref[t, link], which].astype(F32)
-
-        upper = face(1, 1)
-        lower = face(6, 0)
-        left = face(3, 3)
-        right = face(4, 2)
-        corner_ul = face(0, 1)[31:32]
-        corner_ur = face(2, 1)[0:1]
-        corner_dl = face(5, 0)[31:32]
-        corner_dr = face(7, 0)[0:1]
+        halo = halo_r[0, t].astype(F32)
+        for g in range(1, GROUP):
+            halo = halo + halo_r[g, t].astype(F32)
+        upper, lower, left, right = [halo[at * side:(at + 1) * side] for at in range(4)]
+        corners = halo[4 * side:4 * side + 8]
+        corner_ul, corner_ur = corners[0:1], corners[1:2]
+        corner_dl, corner_dr = corners[2:3], corners[3:4]
         for b in range(4):
             part = slice(b * 8, b * 8 + 8)
             above = jnp.concatenate([upper[part], ep[4, b + 1, rows].astype(F32)[0:56]], axis=0)
@@ -276,6 +260,17 @@
         for h in range(GH):
             part = slice(g * GW + h * HD, g * GW + h * HD + HD)
             kv_ref[g, h] = jnp.concatenate([keys[:, part], values[:, part]], axis=1).astype(BF16)
+    for e in range(1, GROUP):
+        n_copy(e).wait_send()
+        h_copy(e).wait_send()
+    for s in range(cols - 1):
+        for k, ok, up, down in stage_blocks(c, cols, s):
+            def body(k=k, up=up, down=down):
+                if up:
+                    when(c + 1 < cols, lambda: z_copy(k, 0).wait_send())
+                if down:
+                    when(c >= 1, lambda: z_copy(k, 1).wait_send())
+            when(ok, body)
 
 
 def attend_kernel(
@@ -405,22 +400,20 @@
     for h in range(GH):
         for d in range(1, GROUP):
             kv_plane(h, d).start()
-        if h == 0:
-            for d in range(1, GROUP):
-                q_plane(d).start()
-    for d in range(1, GROUP):
-        c_plane(d).start()
     z = [z_steps(h) for h in range(GH)]
     grads = [grad_steps(h) for h in range(GH)]
     advance(z[0])
     advance(z[1])
     advance(z[0])
     advance(z[2])
+    for d in range(1, GROUP):
+        q_plane(d).start()
     advance(z[0])
     advance(z[1])
     drain(z[0])
     for d in range(1, GROUP):
         q_plane(d).wait_recv()
+        c_plane(d).start()
     attend(0, 0, 2)
     advance(z[1])
     advance(z[2])
@@ -502,6 +495,7 @@
     ).reshape(tiles, 4, side, ch)
     x = x.reshape(PATCH, PATCH, rows, ch)
 
+    table = jnp.pad(neighbours, ((0, 8 - tiles), (0, 120)))
     tok, kv, q = pl.pallas_call(
         functools.partial(embed_kernel, cols),
         out_shape=(
@@ -509,23 +503,28 @@
             jax.ShapeDtypeStruct((GROUP, GH, rows, 2 * HD), BF16),
             jax.ShapeDtypeStruct((GROUP, rows, GW), BF16),
         ),
-        in_specs=[anyw, vmem, pl.BlockSpec(memory_space=pltpu.SMEM), vmem, anyw, anyw, anyw, anyw],
+        in_specs=[anyw, vmem, vmem, vmem, anyw, anyw, anyw, anyw],
         out_specs=(vmem, vmem, vmem),
         scratch_shapes=[
-            pltpu.VMEM((2 * n + 1, 4, side, ch), BF16),
+            pltpu.VMEM((2 * cols + 1, 4, side, ch), BF16),
+            pltpu.VMEM((GROUP, tiles, 4 * side + 16, ch), BF16),
+            pltpu.VMEM((GROUP, tiles, 4 * side + 16, ch), BF16),
+            pltpu.VMEM((GROUP, 8, 128), jnp.int32),
+            pltpu.SMEM((GROUP, 8, 128), jnp.int32),
             pltpu.VMEM((6, 6, rows, ch), BF16),
             pltpu.VMEM(patch_weight.shape, BF16),
             pltpu.VMEM((3, dm, dm), BF16),
-            dma((6, cols)),
-            dma((5, cols)),
-            dma((5,)),
+            dma((GROUP,)), dma((GROUP,)),
+            dma((2, cols)), dma((cols,)),
+            dma((GROUP,)), dma((GROUP,)),
+            dma((6,)),
         ],
         compiler_params=pltpu.CompilerParams(
             collective_id=0, has_side_effects=True, vmem_limit_bytes=52 * 2**20
         ),
         name="embed",
     )(
-        x, own, neighbours, conv_weight.reshape(9, ch, ch), patch_weight,
+        x, own, table, conv_weight.reshape(9, ch, ch), patch_weight,
         query_weight, key_weight, value_weight,
     )
 

time: 105 us -> 103 us (0.981)
  Pallas kernels: 96.2 us -> 94.1 us
    pallas_call x1, Pallas kernels: 33.7 us -> 31.2 us  [local(): pl.pallas_call(functools.partial(embed_kernel, cols), out_shape=(jax.Shap...]
    unnamed x7 -> x5, local copies, waits for them, and re-layouts: 6.22 us -> 6.21 us
where the time goes in v4:
time: 103 us
  Pallas kernels  94.1 us (91%)
  local copies, waits for them, and re-layouts  8.25 us (8%)
    pallas_call x1, Pallas kernels, local(): pl.pallas_call(functools.partial(attend_kernel, cols, own_rows), out_shap...  62.8 us
    pallas_call x1, Pallas kernels, local(): pl.pallas_call(functools.partial(embed_kernel, cols), out_shape=(jax.Shap...  31.2 us
    unnamed x5, local copies, waits for them, and re-layouts  6.21 us

profile of v4, /device:TPU:0, one launch (start us, length us, event | category | flops | bytes accessed | tf_op | source)
XLA Modules:
  0.0 103.0 jit_solution(5826036653068936119)
XLA Ops:
  0.6 0.7 pad.4.nb_ref
  1.3 2.3 %copy.20 = bf16[2,32,32,256]{3,0,2,1:T(2,128)(2,1)S(1)} copy(bf16[2,32,32,256]{3,2,1,0:T(8,128)(2,1)} %param.9) | data formatting | bytes 2097152 | tf_op args[0]
  3.8 1.2 %copy.21 = bf16[4,4,2,8,8,256]{5,4,3,2,1,0:T(8,128)(2,1)} copy(bf16[4,4,2,8,8,256]{5,2,1,4,0,3:T(2,128)(2,1)S(1)} %bitcast.31) | data formatting | bytes 2097152 | tf_op jit(solution)/shard_map/transpose | solution.py:486
  5.0 0.0 copy-start
  5.0 31.2 %embed.1 = (bf16[128,768]{1,0:T(8,128)(2,1)S(1)}, bf16[4,3,128,128]{3,2,1,0:T(8,128)(2,1)S(1)}, bf16[4,128,192]{2,1,0:T(8,128)(2,1)S(1)}) custom-call(bf16[4,4,128,256]{3,2,1,0:T(8,128)(2,1)} %bitcast.32, bf16[2,4,32,256]{3,2,1,0:T(8,128)(2,1)S(1)} %pad_maximum_fusion.own_ref, s32[8,128]{1,0:T(8,128)S(1)} %pad.4.nb_ref, bf16[9,256,256]{2,1,0:T(8,128)(2,1)} %bitcast.33, ...), custom_call_target="tpu_custom_call" | custom-call | tf_op jit(solution)/shard_map/embed/pallas_call | solution.py:499
  36.3 0.0 copy-done
  36.3 62.8 %attend.1 = (bf16[128,768]{1,0:T(8,128)(2,1)S(1)}, f32[768,768]{1,0:T(8,128)}) custom-call(bf16[128,768]{1,0:T(8,128)(2,1)S(1)} %get-tuple-element.5.tok_ref, bf16[4,3,128,128]{3,2,1,0:T(8,128)(2,1)S(1)} %get-tuple-element.6.kv_ref, bf16[4,128,192]{2,1,0:T(8,128)(2,1)S(1)} %get-tuple-element.7.q_ref, bf16[128,768]{1,0:T(8,128)(2,1)S(1)} %copy-done, ...), custom_call_target="tpu_custom_call" | custom-call | tf_op jit(solution)/shard_map/attend/pallas_call | solution.py:533
  99.1 0.7 copy.40
  99.8 3.2 %copy.41 = f32[768,768]{1,0:T(8,128)} copy(f32[768,768]{1,0:T(8,128)} %get-tuple-element.19) | data formatting | bytes 4718592
  (5 shorter events, 0.1 us)
Async XLA Ops:
  5.0 31.2 %copy-start = (bf16[128,768]{1,0:T(8,128)(2,1)S(1)}, bf16[128,768]{1,0:T(8,128)(2,1)}, u32[]{:S(2)}) copy-start(bf16[128,768]{1,0:T(8,128)(2,1)} %cot_ref.1) | copy-start | bytes 589828

commit v5 on v4

--- a/solution.py
+++ b/solution.py
@@ -49,7 +49,7 @@
     return [(c - s, c - s >= 0, True, False), (c + s, c + s < cols, False, True)]
 
 
-def direct_steps(full, cols, zs, zr, ps, pr):
+def direct_copies(full, cols, zs, zr, ps, pr):
     me, c, p = place()
 
     def z_copy(d, k):
@@ -60,40 +60,13 @@
         k = (c + cols - d) % cols
         return remote(full(k, q), full(k, q), ps(d, e), pr(d, e), c * GROUP + (p + e) % GROUP)
 
-    for d in range(1, cols):
-        z_copy(d, c).start()
-    for e in range(1, GROUP):
-        plane(0, e, p).start()
-    yield
-    for d in range(1, cols):
-        z_copy(d, (c + cols - d) % cols).wait_recv()
-        for e in range(1, GROUP):
-            plane(d, e, p).start()
-    yield
-    for d in range(cols):
-        for e in range(1, GROUP):
-            plane(d, e, (p + GROUP - e) % GROUP).wait_recv()
-    for d in range(cols):
-        if d:
-            z_copy(d, c).wait_send()
-        for e in range(1, GROUP):
-            plane(d, e, p).wait_send()
-
-
-def advance(steps):
-    return next(steps, "end") != "end"
-
-
-def drain(*many):
-    live = list(many)
-    while live:
-        live = [steps for steps in live if advance(steps)]
+    return z_copy, plane
 
 
 def embed_kernel(
     cols, x_ref, own_ref, nb_ref, cw_ref, pw_hbm, wq_hbm, wk_hbm, wv_hbm,
     tok_ref, kv_ref, q_ref,
-    faces, halo_s, halo_r, nb_all, nb_s, ep, pw, ww,
+    faces, halo_s, halo_r, nb_all, nb_s, ep, pw, ww, tok,
     n_ss, n_rs, z_ss, z_rs, h_ss, h_rs, local_sem,
 ):
     me, c, p = place()
@@ -190,10 +163,13 @@
             )
             target[t, 4 * side:4 * side + 16] = corners.astype(BF16)
 
-    for e in range(1, GROUP):
+    def fill_send(e, carry):
         g = (p + e) % GROUP
         fill(g, halo_s.at[g])
         h_copy(e).start()
+        return carry
+
+    lax.fori_loop(1, GROUP, fill_send, 0)
     fill(p, halo_r.at[p])
 
     loads[0].wait()
@@ -233,8 +209,9 @@
             ep[a, 5, rows] = jnp.where(first == 7, spread(rights[a]), east).astype(BF16)
 
     loads[1].wait()
-    tok = jnp.zeros(tok_ref.shape, F32)
-    for i in range(4):
+    tok[...] = jnp.zeros(tok.shape, F32)
+
+    def phase_row(i, carry):
         acc = jnp.zeros((512, ch), F32)
         for dy in range(3):
             for dx in range(3):
@@ -244,10 +221,14 @@
                 )
         hidden = jax.nn.gelu(acc).astype(BF16)
         wide = jnp.concatenate([hidden[j * 128:(j + 1) * 128] for j in range(4)], axis=1)
-        tok = tok + jnp.dot(
-            wide, pw[i * 4 * ch:(i + 1) * 4 * ch], preferred_element_type=F32
-        )
-    tokens = tok.astype(BF16)
+        tok[...] += jnp.dot(
+            wide, pw[pl.ds(pl.multiple_of(i * 4 * ch, 4 * ch), 4 * ch)],
+            preferred_element_type=F32,
+        )
+        return carry
+
+    lax.fori_loop(0, 4, phase_row, 0)
+    tokens = tok[...].astype(BF16)
     tok_ref[...] = tokens
     for load in loads[2:]:
         load.wait()
@@ -255,10 +236,11 @@
     keys = jnp.dot(tokens, ww[1], preferred_element_type=F32)
     values = jnp.dot(tokens, ww[2], preferred_element_type=F32)
     for g in range(GROUP):
-        part = slice(g * GW, (g + 1) * GW)
-        q_ref[g] = query[:, part].astype(BF16)
         for h in range(GH):
             part = slice(g * GW + h * HD, g * GW + h * HD + HD)
+            q_ref[g, h] = jnp.concatenate(
+                [query[:, part], jnp.zeros((query.shape[0], HD), F32)], axis=1
+            ).astype(BF16)
             kv_ref[g, h] = jnp.concatenate([keys[:, part], values[:, part]], axis=1).astype(BF16)
     for e in range(1, GROUP):
         n_copy(e).wait_send()
@@ -276,7 +258,7 @@
 def attend_kernel(
     cols, own_rows, tok_ref, kv_ref, q_ref, cot_ref, wo_ref,
     mixed_ref, grad_ref,
-    kvg, qg, og, ogr, cotg, part_f, part_s, part_r, gr,
+    kvg, qg, og, ogr, cotg, part_f, part_s, part_r, gr, mix,
     kv_ss, kv_rs, q_ss, q_rs, c_ss, c_rs, o_ss, o_rs, z_ss, z_rs, p_ss, p_rs, zs, zr, ss, rs,
 ):
     n = cols * GROUP
@@ -320,30 +302,23 @@
         to = c + 1 - 2 * way
         return remote(block, block, z_ss.at[h, way, k], z_rs.at[h, k], to * GROUP + p)
 
-    def z_steps(h):
-        for d in range(1, GROUP):
-            kv_plane(h, d).wait_recv()
-        for s in range(cols):
-            for k, ok, up, down in stage_blocks(c, cols, s):
-                def body(k=k, up=up, down=down):
-                    if s > 0:
-                        z_copy(h, k, 0).wait_recv()
-                    if s < cols - 1:
-                        if up:
-                            when(c + 1 < cols, lambda: z_copy(h, k, 0).start())
-                        if down:
-                            when(c >= 1, lambda: z_copy(h, k, 1).start())
-                when(ok, body)
-            yield
+    def z_stage(h, s):
+        for k, ok, up, down in stage_blocks(c, cols, s):
+            def body(k=k, up=up, down=down):
+                if s > 0:
+                    z_copy(h, k, 0).wait_recv()
+                if s < cols - 1:
+                    if up:
+                        when(c + 1 < cols, lambda: z_copy(h, k, 0).start())
+                    if down:
+                        when(c >= 1, lambda: z_copy(h, k, 1).start())
+            when(ok, body)
 
     factor = HD ** (-0.5) * math.log2(math.e)
 
-    def attend(h, first, last):
-        lanes = slice(h * HD, (h + 1) * HD)
-        count = (last - first) * 128
+    def attend(h, i):
         both = kvg[h].reshape(n * 128, 2 * HD)
-        query = qg[first:last, :, lanes].reshape(count, HD)
-        query = jnp.concatenate([query, jnp.zeros_like(query)], axis=1)
+        query = qg[pl.ds(2 * i, 2), h].reshape(256, 2 * HD)
         scores = lax.dot_general(
             query, both, (((1,), (1,)), ((), ())), preferred_element_type=F32
         )
@@ -351,8 +326,7 @@
         weights = jnp.exp2((scores - top) * factor)
         total = jnp.sum(weights, axis=1, keepdims=True)
         out = jnp.dot(weights.astype(BF16), both, preferred_element_type=F32)
-        out = (out / total)[:, HD:].astype(BF16)
-        og[first:last, :, lanes] = out.reshape(last - first, 128, HD)
+        og[pl.ds(2 * i, 2), h] = (out / total).astype(BF16).reshape(2, 128, 2 * HD)
 
     def p_copy(h, d):
         j = (c + d) % cols
@@ -360,19 +334,19 @@
             part_s.at[h, j], part_r.at[h, d], p_ss.at[h, d], p_rs.at[h, d], j * GROUP + p
         )
 
-    def grad_steps(h):
+    def partial(h):
         part = lax.dot_general(
-            og[:, :, h * HD:(h + 1) * HD].reshape(GROUP * 128, HD),
+            og[:, h].reshape(GROUP * 128, 2 * HD),
             cotg[...].reshape(GROUP * 128, -1),
             (((0,), (0,)), ((), ())), preferred_element_type=F32,
-        ).reshape(owners, own_rows, -1)
+        )[HD:].reshape(owners, own_rows, -1)
         part_f[h] = part
         part_s[h] = part.astype(BF16)
         for d in range(1, cols):
             j, copy = p_copy(h, d)
             when(j < owners if owners < cols else True, copy.start)
-        yield
-
+
+    def collect(h):
         def reduce():
             acc = part_f[h, c]
             for d in range(1, cols):
@@ -388,65 +362,117 @@
             pl.when(c >= owners)(nothing)
         else:
             reduce()
-        yield from direct_steps(
+        g_copies = gather_copies(h)
+        for d in range(1, cols):
+            g_copies[0](d, c).start()
+        for e in range(1, GROUP):
+            g_copies[1](0, e, p).start()
+
+    def gather_copies(h):
+        return direct_copies(
             lambda k, q: gr.at[h, k * GROUP + q], cols,
             lambda d: zs.at[h, d], lambda d: zr.at[h, d],
             lambda d, e: ss.at[h, d, e], lambda d, e: rs.at[h, d, e],
         )
+
+    def spread_plane(h):
+        z_part, plane = gather_copies(h)
         for d in range(1, cols):
-            j, copy = p_copy(h, d)
-            when(j < owners if owners < cols else True, copy.wait_send)
+            z_part(d, (c + cols - d) % cols).wait_recv()
+            for e in range(1, GROUP):
+                plane(d, e, p).start()
+
+    def finish(h, carry):
+        z_part, plane = gather_copies(h)
+        for d in range(cols):
+            for e in range(1, GROUP):
+                plane(d, e, (p + GROUP - e) % GROUP).wait_recv()
+        for d in range(cols):
+            if d:
+                z_part(d, c).wait_send()
+                j, copy = p_copy(h, d)
+                when(j < owners if owners < cols else True, copy.wait_send)
+            for e in range(1, GROUP):
+                plane(d, e, p).wait_send()
+        return carry
 
     for h in range(GH):
         for d in range(1, GROUP):
             kv_plane(h, d).start()
-    z = [z_steps(h) for h in range(GH)]
-    grads = [grad_steps(h) for h in range(GH)]
-    advance(z[0])
-    advance(z[1])
-    advance(z[0])
-    advance(z[2])
     for d in range(1, GROUP):
         q_plane(d).start()
-    advance(z[0])
-    advance(z[1])
-    drain(z[0])
+    for h in range(GH):
+        for d in range(1, GROUP):
+            kv_plane(h, d).wait_recv()
+        z_stage(h, 0)
+    for d in range(1, GROUP):
+        c_plane(d).start()
+    z_stage(0, 1)
+    z_stage(0, 2)
     for d in range(1, GROUP):
         q_plane(d).wait_recv()
-        c_plane(d).start()
-    attend(0, 0, 2)
-    advance(z[1])
-    advance(z[2])
-    attend(0, 2, 4)
-    drain(z[1])
-    advance(z[2])
-    for d in range(1, GROUP):
-        c_plane(d).wait_recv()
-    advance(grads[0])
-    attend(1, 0, 2)
-    drain(z[2])
-    advance(grads[0])
-    attend(1, 2, 4)
-    advance(grads[0])
-    advance(grads[1])
-    attend(2, 0, 2)
-    advance(grads[1])
-    attend(2, 2, 4)
-    for d in range(1, GROUP):
-        o_plane(d).start()
-    advance(grads[2])
-    advance(grads[1])
+
+    def head(h, carry):
+        for s in range(3, cols):
+            z_stage(h, s)
+
+        @pl.when(h + 1 < GH)
+        def _():
+            z_stage(h + 1, 1)
+
+        def half(i, inner):
+            @pl.when((i == 1) & (h + 1 < GH))
+            def _():
+                z_stage(h + 1, 2)
+
+            @pl.when((i == 1) & (h >= 1))
+            def _():
+                collect(h - 1)
+
+            attend(h, i)
+            return inner
+
+        lax.fori_loop(0, 2, half, 0)
+
+        @pl.when(h == 0)
+        def _():
+            for d in range(1, GROUP):
+                c_plane(d).wait_recv()
+
+        @pl.when(h == GH - 1)
+        def _():
+            for d in range(1, GROUP):
+                o_plane(d).start()
+
+        partial(h)
+
+        @pl.when(h >= 1)
+        def _():
+            spread_plane(h - 1)
+
+        return carry
+
+    lax.fori_loop(0, GH, head, 0)
     ogr[p] = og[p]
     for d in range(1, GROUP):
         o_plane(d).wait_recv()
-    total = tok_ref[...].astype(F32)
-    for g in range(GROUP):
-        total = total + jnp.dot(
-            ogr[g], wo_ref[g * GW:(g + 1) * GW], preferred_element_type=F32
-        )
-    mixed_ref[...] = total.astype(BF16)
-    advance(grads[2])
-    drain(grads[0], grads[1], grads[2])
+    mix[...] = tok_ref[...].astype(F32)
+
+    def mix_group(g, carry):
+        total = mix[...]
+        for h in range(GH):
+            weight = wo_ref[pl.ds(pl.multiple_of(g * GW + h * HD, HD), HD)]
+            total = total + jnp.dot(
+                ogr[g, h][:, HD:], weight, preferred_element_type=F32
+            )
+        mix[...] = total
+        return carry
+
+    collect(GH - 1)
+    lax.fori_loop(0, GROUP, mix_group, 0)
+    mixed_ref[...] = mix[...].astype(BF16)
+    spread_plane(GH - 1)
+    lax.fori_loop(0, GH, finish, 0)
     for q in range(GROUP):
         for h in range(GH):
             for k in range(owners):
@@ -501,7 +527,7 @@
         out_shape=(
             jax.ShapeDtypeStruct((rows, dm), BF16),
             jax.ShapeDtypeStruct((GROUP, GH, rows, 2 * HD), BF16),
-            jax.ShapeDtypeStruct((GROUP, rows, GW), BF16),
+            jax.ShapeDtypeStruct((GROUP, GH, rows, 2 * HD), BF16),
         ),
         in_specs=[anyw, vmem, vmem, vmem, anyw, anyw, anyw, anyw],
         out_specs=(vmem, vmem, vmem),
@@ -514,6 +540,7 @@
             pltpu.VMEM((6, 6, rows, ch), BF16),
             pltpu.VMEM(patch_weight.shape, BF16),
             pltpu.VMEM((3, dm, dm), BF16),
+            pltpu.VMEM((rows, dm), F32),
             dma((GROUP,)), dma((GROUP,)),
             dma((2, cols)), dma((cols,)),
             dma((GROUP,)), dma((GROUP,)),
@@ -540,14 +567,15 @@
         out_specs=(vmem, vmem),
         scratch_shapes=[
             pltpu.VMEM((GH, n, rows, 2 * HD), BF16),
-            pltpu.VMEM((GROUP, rows, GW), BF16),
-            pltpu.VMEM((GROUP, rows, GW), BF16),
-            pltpu.VMEM((GROUP, rows, GW), BF16),
+            pltpu.VMEM((GROUP, GH, rows, 2 * HD), BF16),
+            pltpu.VMEM((GROUP, GH, rows, 2 * HD), BF16),
+            pltpu.VMEM((GROUP, GH, rows, 2 * HD), BF16),
             pltpu.VMEM((GROUP, rows, dm), BF16),
             pltpu.VMEM((GH, owners, own_rows, dm), F32),
             pltpu.VMEM((GH, owners, own_rows, dm), BF16),
             pltpu.VMEM((GH, cols, own_rows, dm), BF16),
             pltpu.VMEM((GH, n, own_rows, dm), BF16),
+            pltpu.VMEM((rows, dm), F32),
             dma((GH, GROUP)), dma((GH, GROUP)),
             dma((GROUP,)), dma((GROUP,)),
             dma((GROUP,)), dma((GROUP,)),

time: 103 us -> 98.7 us (0.958)
  Pallas kernels: 94.1 us -> 89.5 us
    pallas_call x1, Pallas kernels: 62.8 us -> 57.6 us  [local(): pl.pallas_call(functools.partial(attend_kernel, cols, own_rows), out_shap...]
where the time goes in v5:
time: 98.7 us; the launch traced here: 98.4 us
  Pallas kernels  89.5 us (91%)
  local copies, waits for them, and re-layouts  8.25 us (8%)
    pallas_call x1, Pallas kernels, local(): pl.pallas_call(functools.partial(attend_kernel, cols, own_rows), out_shap...  57.6 us
    pallas_call x1, Pallas kernels, local(): pl.pallas_call(functools.partial(embed_kernel, cols), out_shape=(jax.Shap...  31.8 us
    unnamed x5, local copies, waits for them, and re-layouts  6.21 us

profile of v5, /device:TPU:0, one launch (start us, length us, event | category | flops | bytes accessed | tf_op | source)
XLA Modules:
  0.0 98.4 jit_solution(2404174603989925877)
XLA Ops:
  0.6 0.7 pad.4.nb_ref
  1.3 2.3 %copy.20 = bf16[2,32,32,256]{3,0,2,1:T(2,128)(2,1)S(1)} copy(bf16[2,32,32,256]{3,2,1,0:T(8,128)(2,1)} %param.9) | data formatting | bytes 2097152 | tf_op args[0]
  3.8 1.2 %copy.21 = bf16[4,4,2,8,8,256]{5,4,3,2,1,0:T(8,128)(2,1)} copy(bf16[4,4,2,8,8,256]{5,2,1,4,0,3:T(2,128)(2,1)S(1)} %bitcast.31) | data formatting | bytes 2097152 | tf_op jit(solution)/shard_map/transpose | solution.py:512
  5.0 0.0 copy-start
  5.0 31.8 %embed.1 = (bf16[128,768]{1,0:T(8,128)(2,1)S(1)}, bf16[4,3,128,128]{3,2,1,0:T(8,128)(2,1)S(1)}, bf16[4,3,128,128]{3,2,1,0:T(8,128)(2,1)S(1)}) custom-call(bf16[4,4,128,256]{3,2,1,0:T(8,128)(2,1)} %bitcast.32, bf16[2,4,32,256]{3,2,1,0:T(8,128)(2,1)S(1)} %pad_maximum_fusion.own_ref, s32[8,128]{1,0:T(8,128)S(1)} %pad.4.nb_ref, bf16[9,256,256]{2,1,0:T(8,128)(2,1)} %bitcast.33, ...), custom_call_target="tpu_custom_call" | custom-call | tf_op jit(solution)/shard_map/embed/pallas_call | solution.py:525
  36.9 0.0 copy-done
  36.9 57.6 %attend.1 = (bf16[128,768]{1,0:T(8,128)(2,1)S(1)}, f32[768,768]{1,0:T(8,128)}) custom-call(bf16[128,768]{1,0:T(8,128)(2,1)S(1)} %get-tuple-element.5.tok_ref, bf16[4,3,128,128]{3,2,1,0:T(8,128)(2,1)S(1)} %get-tuple-element.6.kv_ref, bf16[4,3,128,128]{3,2,1,0:T(8,128)(2,1)S(1)} %get-tuple-element.7.q_ref, bf16[128,768]{1,0:T(8,128)(2,1)S(1)} %copy-done, ...), custom_call_target="tpu_custom_call" | custom-call | tf_op jit(solution)/shard_map/attend/pallas_call | solution.py:560
  94.5 0.7 copy.40
  95.2 3.2 %copy.41 = f32[768,768]{1,0:T(8,128)} copy(f32[768,768]{1,0:T(8,128)} %get-tuple-element.19) | data formatting | bytes 4718592
  (5 shorter events, 0.1 us)
Async XLA Ops:
  5.0 31.9 %copy-start = (bf16[128,768]{1,0:T(8,128)(2,1)S(1)}, bf16[128,768]{1,0:T(8,128)(2,1)}, u32[]{:S(2)}) copy-start(bf16[128,768]{1,0:T(8,128)(2,1)} %cot_ref.1) | copy-start | bytes 589828

commit v6 on v5

--- a/solution.py
+++ b/solution.py
@@ -95,7 +95,8 @@
         load.start()
     faces[pl.ds(2 * c, 2)] = own_ref[...]
     faces[2 * cols] = jnp.zeros(faces.shape[1:], BF16)
-    nb_all[p] = nb_ref[...]
+    nb_all[p] = jnp.zeros(nb_all.shape[1:], jnp.int32)
+    nb_all[p, 0:nb_ref.shape[0], 0:nb_ref.shape[1]] = nb_ref[...]
     inner = (c >= 1) & (c + 1 < cols)
 
     @pl.when(inner)
@@ -477,7 +478,7 @@
         for h in range(GH):
             for k in range(owners):
                 row = q * GW + h * HD + k * own_rows
-                grad_ref[row:row + own_rows] = gr[h, k * GROUP + q].astype(F32)
+                grad_ref[row:row + own_rows] = gr[h, k * GROUP + q]
 
     for d in range(1, GROUP):
         for h in range(GH):
@@ -496,6 +497,11 @@
                 when(ok, body)
 
 
+def widen_kernel(mixed_ref, grad_ref, mixed_out, grad_out):
+    mixed_out[...] = mixed_ref[...]
+    grad_out[...] = grad_ref[...].astype(F32)
+
+
 def local(
     n, features, neighbours, conv_weight, patch_weight, query_weight, key_weight,
     value_weight, output_weight, cotangent,
@@ -521,7 +527,6 @@
     ).reshape(tiles, 4, side, ch)
     x = x.reshape(PATCH, PATCH, rows, ch)
 
-    table = jnp.pad(neighbours, ((0, 8 - tiles), (0, 120)))
     tok, kv, q = pl.pallas_call(
         functools.partial(embed_kernel, cols),
         out_shape=(
@@ -551,7 +556,7 @@
         ),
         name="embed",
     )(
-        x, own, table, conv_weight.reshape(9, ch, ch), patch_weight,
+        x, own, neighbours, conv_weight.reshape(9, ch, ch), patch_weight,
         query_weight, key_weight, value_weight,
     )
 
@@ -561,7 +566,7 @@
         functools.partial(attend_kernel, cols, own_rows),
         out_shape=(
             jax.ShapeDtypeStruct((rows, dm), BF16),
-            jax.ShapeDtypeStruct((dm, dm), F32),
+            jax.ShapeDtypeStruct((dm, dm), BF16),
         ),
         in_specs=[vmem] * 5,
         out_specs=(vmem, vmem),
@@ -590,7 +595,19 @@
         ),
         name="attend",
     )(tok, kv, q, cotangent, output_weight)
-    return mixed, grad
+    whole = pl.BlockSpec((rows, dm), lambda i: (0, 0))
+    third = pl.BlockSpec((dm // 3, dm), lambda i: (i, 0))
+    return pl.pallas_call(
+        widen_kernel,
+        grid=(3,),
+        out_shape=(
+            jax.ShapeDtypeStruct((rows, dm), BF16),
+            jax.ShapeDtypeStruct((dm, dm), F32),
+        ),
+        in_specs=[whole, third],
+        out_specs=(whole, third),
+        name="widen",
+    )(mixed, grad)
 
 
 def solution(mesh):

time: 98.7 us -> 97.8 us (level)
  local copies, waits for them, and re-layouts: 8.25 us -> 4.35 us
  Pallas kernels: 89.5 us -> 92.4 us
    pallas_call x0 -> x1, Pallas kernels: none -> 3.42 us  [local(): pl.pallas_call(widen_kernel, grid=(3,), out_shape=(jax.ShapeDtypeStruct((...]
    unnamed x5 -> x7, local copies, waits for them, and re-layouts: 6.21 us -> 3.01 us
where the time goes in v6:
time: 97.8 us; the launch traced here: 97.5 us
  Pallas kernels  92.4 us (94%)
  local copies, waits for them, and re-layouts  4.35 us (4%)
    pallas_call x1, Pallas kernels, local(): pl.pallas_call(functools.partial(attend_kernel, cols, own_rows), out_shap...  57.2 us
    pallas_call x1, Pallas kernels, local(): pl.pallas_call(functools.partial(embed_kernel, cols), out_shape=(jax.Shap...  31.8 us
    pallas_call x1, Pallas kernels, local(): pl.pallas_call(widen_kernel, grid=(3,), out_shape=(jax.ShapeDtypeStruct((...  3.42 us
    unnamed x7, local copies, waits for them, and re-layouts  3.01 us

profile of v6, /device:TPU:0, one launch (start us, length us, event | category | flops | bytes accessed | tf_op | source)
XLA Modules:
  0.0 97.5 jit_solution(3807386065496646988)
XLA Ops:
  0.6 2.3 %copy.20 = bf16[2,32,32,256]{3,0,2,1:T(2,128)(2,1)S(1)} copy(bf16[2,32,32,256]{3,2,1,0:T(8,128)(2,1)} %param.9) | data formatting | bytes 2097152 | tf_op args[0]
  3.1 0.0 copy-start.2
  3.1 1.2 %copy.21 = bf16[4,4,2,8,8,256]{5,4,3,2,1,0:T(8,128)(2,1)} copy(bf16[4,4,2,8,8,256]{5,2,1,4,0,3:T(2,128)(2,1)S(1)} %bitcast.31) | data formatting | bytes 2097152 | tf_op jit(solution)/shard_map/transpose | solution.py:518
  4.4 0.0 copy-done.2
  4.4 0.0 copy-start
  4.4 31.8 %embed.1 = (bf16[128,768]{1,0:T(8,128)(2,1)S(1)}, bf16[4,3,128,128]{3,2,1,0:T(8,128)(2,1)S(1)}, bf16[4,3,128,128]{3,2,1,0:T(8,128)(2,1)S(1)}) custom-call(bf16[4,4,128,256]{3,2,1,0:T(8,128)(2,1)} %bitcast.32, bf16[2,4,32,256]{3,2,1,0:T(8,128)(2,1)S(1)} %pad_maximum_fusion.own_ref, s32[2,8]{1,0:T(2,128)S(1)} %copy-done.2, bf16[9,256,256]{2,1,0:T(8,128)(2,1)} %bitcast.33, ...), custom_call_target="tpu_custom_call" | custom-call | tf_op jit(solution)/shard_map/embed/pallas_call | solution.py:530
  36.2 0.0 copy-done
  36.2 57.2 %attend.1 = (bf16[128,768]{1,0:T(8,128)(2,1)S(1)}, bf16[768,768]{1,0:T(8,128)(2,1)}) custom-call(bf16[128,768]{1,0:T(8,128)(2,1)S(1)} %get-tuple-element.7.tok_ref, bf16[4,3,128,128]{3,2,1,0:T(8,128)(2,1)S(1)} %get-tuple-element.8.kv_ref, bf16[4,3,128,128]{3,2,1,0:T(8,128)(2,1)S(1)} %get-tuple-element.9.q_ref, bf16[128,768]{1,0:T(8,128)(2,1)S(1)} %copy-done, ...), custom_call_target="tpu_custom_call" | custom-call | tf_op jit(solution)/shard_map/attend/pallas_call | solution.py:565
  93.4 0.0 copy-start.1
  93.4 0.7 copy-done.1
  94.1 3.4 %widen.1 = (bf16[128,768]{1,0:T(8,128)(2,1)}, f32[768,768]{1,0:T(8,128)}) custom-call(bf16[128,768]{1,0:T(8,128)(2,1)} %copy-done.1, bf16[768,768]{1,0:T(8,128)(2,1)} %get-tuple-element.11.grad_ref), custom_call_target="tpu_custom_call" | custom-call | tf_op jit(solution)/shard_map/widen/pallas_call | solution.py:600
  (5 shorter events, 0.1 us)
Async XLA Ops:
  3.1 1.3 %copy-start.2 = (s32[2,8]{1,0:T(2,128)S(1)}, s32[2,8]{1,0:T(2,128)}, u32[]{:S(2)}) copy-start(s32[2,8]{1,0:T(2,128)} %nb_ref.1) | copy-start | bytes 196
  4.4 31.9 %copy-start = (bf16[128,768]{1,0:T(8,128)(2,1)S(1)}, bf16[128,768]{1,0:T(8,128)(2,1)}, u32[]{:S(2)}) copy-start(bf16[128,768]{1,0:T(8,128)(2,1)} %cot_ref.1) | copy-start | bytes 589828
  93.4 0.7 copy-start.1
